TPU v7x, 512 devices: a whole 4x8x8 slice. The times are simulated.
512 devices in a mesh: region: 16 (over y, core), tile: 32 (over x, z).
Axes of the slice: x: 4, y: 8, z: 8, core: 2. Of those that a mesh axis runs over, the one named last changes fastest.
Arguments:
- prior_pressure: float32 [64, 4, 64, 4096], P(None, None, 'region', 'tile'), may hold values from -6 to 6
- infiltration_source: float32 [64, 64, 4096], P(None, 'region', 'tile'), may hold values from -6 to 6
- soil_class: int32 [4, 64, 4096], P(None, 'region', 'tile'), may hold values from 0 to 11
- soil_k: float32 [12], replicated, may hold values from 0.02 to 0.2
- obs_index: int32 [131072], P(('region', 'tile')), may hold values from 0 to 2047
- obs_value: float32 [131072], P(('region', 'tile')), may hold values from -6 to 6
- obs_var: float32 [131072], P(('region', 'tile')), may hold values from 0.5 to 8
- obs_count: int32 [512], P(('region', 'tile')), may hold values from 1 to 256, as said below
Outputs:
- analysis: float32 [64, 4, 64, 4096], P(None, None, 'region', 'tile')
Inputs may be any that keep to these rules, and one draw needn't show every extreme that they name: `obs_count`: at least one block has all 256 slots live.
All inputs are finite; a program needn't handle non-finite values.
Results may differ from a plain program's by a relative error of at most 0.00019.
Values sent between devices are 32-bit elements; how exact they have to be, the bound alone decides.
No kernel may reach another device: no remote copies, remote signals or barrier semaphores. Data moves between devices by JAX's collectives and lax.ppermute only.
A program may use at most 64 MiB of HBM per device.

v0:
```python
import jax
import jax.numpy as jnp
from jax import lax
from jax.sharding import PartitionSpec as P

STEPS = 3


step_dt = 0.25
vert_share = 0.5


def extended(block, sides, width):
    for axis, dim in sides:
        count = lax.axis_size(axis)
        forward = [(i, i + 1) for i in range(count - 1)]
        backward = [(target, source) for source, target in forward]
        low = lax.ppermute(
            lax.slice_in_dim(block, block.shape[dim] - width, None, axis=dim), axis, forward
        )
        high = lax.ppermute(lax.slice_in_dim(block, 0, width, axis=dim), axis, backward)
        block = jnp.concatenate([low, block, high], axis=dim)
    return block


def lookup(soil_class, soil_k):
    total = jnp.zeros(soil_class.shape, jnp.float32)
    for index in range(soil_k.shape[0]):
        total = total + jnp.where(soil_class == index, soil_k[index], 0.0)
    return total


def cholesky_lower(matrix):
    order = matrix.shape[0]
    places = jnp.arange(order, dtype=jnp.int32)

    def column_step(column, lower):
        onehot = (places == column.astype(jnp.int32)).astype(matrix.dtype)
        row_now = jnp.dot(onehot, lower, precision=lax.Precision.HIGHEST)
        remain = jnp.dot(matrix, onehot, precision=lax.Precision.HIGHEST) - jnp.dot(
            lower, row_now, precision=lax.Precision.HIGHEST
        )
        pivot = jnp.sqrt(jnp.sum(remain * onehot))
        fresh = jnp.where(
            places >= column.astype(jnp.int32), remain / pivot, jnp.zeros_like(remain)
        )
        return lower + fresh[:, None] * onehot[None, :]

    return lax.fori_loop(0, order, column_step, jnp.zeros_like(matrix))


def lower_inverse(lower):
    order = lower.shape[0]
    places = jnp.arange(order, dtype=jnp.int32)

    def row_step(row, solved):
        onehot = (places == row.astype(jnp.int32)).astype(lower.dtype)
        row_now = jnp.dot(onehot, lower, precision=lax.Precision.HIGHEST)
        pivot = jnp.sum(row_now * onehot)
        fresh = (onehot - jnp.dot(row_now, solved, precision=lax.Precision.HIGHEST)) / pivot
        return solved + onehot[:, None] * fresh[None, :]

    return lax.fori_loop(0, order, row_step, jnp.zeros_like(lower))


def update(padded, bordered_permeability, push):
    cond = bordered_permeability[None] * (0.5 + jax.nn.sigmoid(padded))
    center = padded[:, :, 1:-1, 1:-1]
    kcen = cond[:, :, 1:-1, 1:-1]
    flux = jnp.zeros_like(center)
    for rows, cols in (
        (slice(2, None), slice(1, -1)),
        (slice(None, -2), slice(1, -1)),
        (slice(1, -1), slice(2, None)),
        (slice(1, -1), slice(None, -2)),
    ):
        flux = flux + 0.5 * (kcen + cond[:, :, rows, cols]) * (padded[:, :, rows, cols] - center)
    upward = vert_share * 0.5 * (kcen[:, 1:] + kcen[:, :-1]) * (center[:, 1:] - center[:, :-1])
    flux = (
        flux
        + jnp.pad(upward, ((0, 0), (0, 1), (0, 0), (0, 0)))
        - jnp.pad(upward, ((0, 0), (1, 0), (0, 0), (0, 0)))
    )
    flux = flux + jnp.pad(push[:, None], ((0, 0), (0, center.shape[1] - 1), (0, 0), (0, 0)))
    return center + step_dt * flux


def propagate_pressure(state, bordered_permeability, infiltration_source):
    padded = extended(state, (("region", 2), ("tile", 3)), 1)
    return update(padded, bordered_permeability, infiltration_source)


def shards(
    prior_pressure,
    infiltration_source,
    soil_class,
    soil_k,
    obs_index,
    obs_value,
    obs_var,
    obs_count,
):
    realization_vectors = prior_pressure.shape[0]
    depth = 1
    bordered_permeability = extended(
        lookup(soil_class, soil_k), (("region", 1), ("tile", 2)), depth
    )
    predicted_pressure = prior_pressure
    for step in range(STEPS):
        predicted_pressure = propagate_pressure(
            predicted_pressure, bordered_permeability, infiltration_source
        )
    unrolled_vector = predicted_pressure.reshape(realization_vectors, -1)
    measured_pressure = jnp.take(unrolled_vector, obs_index, axis=1)
    live = (jnp.arange(obs_index.shape[0], dtype=jnp.int32) < obs_count[0]).astype(jnp.float32)
    weight = live / jnp.sqrt(obs_var)
    hmean = jnp.mean(measured_pressure, axis=0)
    anomal = (measured_pressure - hmean) * weight
    innov = (obs_value - hmean) * weight
    gram = jnp.dot(anomal, anomal.T, precision=lax.Precision.HIGHEST)
    bvec = jnp.dot(anomal, innov, precision=lax.Precision.HIGHEST)
    eye = jnp.eye(realization_vectors, dtype=jnp.float32)
    gram, bvec = lax.psum((gram, bvec), ("region", "tile"))
    lower = cholesky_lower((realization_vectors - 1.0) * eye + gram)
    inverse = lower_inverse(lower)
    wmean = jnp.dot(
        inverse.T,
        jnp.dot(inverse, bvec, precision=lax.Precision.HIGHEST),
        precision=lax.Precision.HIGHEST,
    )
    wroot = inverse.T * jnp.sqrt(realization_vectors - 1.0)
    blending_factor = wroot + wmean[:, None]
    sample_average = jnp.mean(predicted_pressure, axis=0)
    deviation_matrix = (predicted_pressure - sample_average).reshape(realization_vectors, -1)
    propagated_vector = jnp.dot(
        blending_factor.T, deviation_matrix, precision=lax.Precision.HIGHEST
    ).reshape(predicted_pressure.shape)
    return sample_average + propagated_vector


def solution(mesh):
    return jax.shard_map(
        shards,
        mesh=mesh,
        in_specs=(
            P(None, None, "region", "tile"),
            P(None, "region", "tile"),
            P(None, "region", "tile"),
            P(),
            P(("region", "tile")),
            P(("region", "tile")),
            P(("region", "tile")),
            P(("region", "tile")),
        ),
        out_specs=P(None, None, "region", "tile"),
        check_vma=False,
    )
```

profile of v0, /device:TPU:1, one launch (start us, length us, event | category | flops | bytes accessed | tf_op | source)
XLA Modules:
  0.0 435.6 jit_solution(1766568834195470314)
XLA Ops:
  0.0 1.8 fusion.141
  1.8 8.3 %select_add_fusion.1 = f32[4,4,128]{2,1,0:T(4,128)S(1)} fusion(s32[4,4,128]{2,1,0:T(4,128)} %param.14, f32[]{:T(128)} %bitcast.11, f32[]{:T(128)} %bitcast.10, f32[]{:T(128)} %bitcast.9, f32[]{:T(128)} %bitcast.8, f32[]{:T(128)} %bitcast.7, f32[]{:T(128)} %bitcast.6, f32[]{:T(128)} %bitcast.5, f32[]{:T(128)} %bitcast.4, f32[]{:T(128)} %bitcast.3, ...), kind=kLoop, calls=%fused_computation.194 | loop fusion | flops 71680 | bytes 16432 | tf_op jit(solution)/shard_map/add | solution.py:29
  10.1 4.6 %collective-permute-start = (f32[4,1,128]{2,1,0:T(1,128)S(1)}, f32[4,1,128]{2,1,0:T(1,128)S(1)}, u32[]{:S(2)}, u32[]{:S(2)}) collective-permute-start(f32[4,1,128]{2,1,0:T(1,128)S(1)} %get-tuple-element.244), channel_id=1, source_target_pairs={{0,32},{32,64},{64,96},{96,128},{128,160},{160,192},{192,224},{224... | collective-permute-start | bytes 6152 | tf_op jit(solution)/shard_map/ppermute | solution.py:18
  14.7 5.5 %collective-permute-start.1 = (f32[4,1,128]{2,1,0:T(1,128)S(1)}, f32[4,1,128]{2,1,0:T(1,128)S(1)}, u32[]{:S(2)}, u32[]{:S(2)}) collective-permute-start(f32[4,1,128]{2,1,0:T(1,128)S(1)} %get-tuple-element.245), channel_id=1, source_target_pairs={{32,0},{64,32},{96,64},{128,96},{160,128},{192,160},{224,192},{256... | collective-permute-start | bytes 6152 | tf_op jit(solution)/shard_map/ppermute | solution.py:21
  20.2 1.2 copy.59
  21.4 1.9 collective-permute-start.4
  23.3 2.4 collective-permute-start.5
  26.5 2.3 collective-permute-start.2
  28.8 1.3 collective-permute-start.3
  32.0 4.1 collective-permute-start.6
  36.3 1.3 collective-permute-start.7
  38.8 2.6 collective-permute-done.7
  43.5 1.0 fusion.48
  44.5 5.1 %collective-permute-start.8 = (f32[64,4,1,128]{3,0,2,1:T(8,128)S(1)}, f32[64,4,1,128]{3,0,2,1:T(8,128)S(1)}, u32[]{:S(2)}, u32[]{:S(2)}) collective-permute-start(f32[64,4,1,128]{3,0,2,1:T(8,128)S(1)} %get-tuple-element.238), channel_id=1, source_target_pairs={{0,32},{32,64},{64,96},{96,128},{128,160},{160,192},{192,224},{224... | collective-permute-start | bytes 393224 | tf_op jit(solution)/shard_map/ppermute | solution.py:18
  49.6 1.9 collective-permute-start.9
  51.5 4.3 collective-permute-done.9
  56.6 5.2 %collective-permute-start.10 = (f32[64,4,6,1]{0,1,3,2:T(4,128)S(1)}, f32[64,4,6,1]{0,1,3,2:T(4,128)S(1)}, u32[]{:S(2)}, u32[]{:S(2)}) collective-permute-start(f32[64,4,6,1]{0,1,3,2:T(4,128)S(1)} %copy.60), channel_id=1, source_target_pairs={{0,1},{1,2},{2,3},{3,4},{4,5},{5,6},{6,7},{7,8},{8,9},{9,10},{10,1... | collective-permute-start | bytes 18440 | tf_op jit(solution)/shard_map/ppermute | solution.py:18
  62.1 1.3 collective-permute-start.11
  63.7 4.3 collective-permute-done.11
  69.4 1.0 fusion.50
  70.4 2.9 collective-permute-start.12
  73.4 1.9 collective-permute-start.13
  75.3 4.3 collective-permute-done.13
  80.3 4.9 %collective-permute-start.14 = (f32[64,4,6,1]{0,1,3,2:T(4,128)S(1)}, f32[64,4,6,1]{0,1,3,2:T(4,128)S(1)}, u32[]{:S(2)}, u32[]{:S(2)}) collective-permute-start(f32[64,4,6,1]{0,1,3,2:T(4,128)S(1)} %copy.66), channel_id=1, source_target_pairs={{0,1},{1,2},{2,3},{3,4},{4,5},{5,6},{6,7},{7,8},{8,9},{9,10},{10,1... | collective-permute-start | bytes 18440 | tf_op jit(solution)/shard_map/ppermute | solution.py:18
  85.5 1.3 collective-permute-start.15
  87.8 2.4 collective-permute-done.15
  91.5 1.1 fusion.131
  94.9 106.0 %all-reduce.7 = (f32[64,64]{1,0:T(8,128)S(1)}, f32[64]{0:T(128)S(1)}) all-reduce(f32[64,64]{1,0:T(8,128)S(1)} %fusion.112, f32[64]{0:T(128)S(1)} %convolution_bitcast_fusion.6), channel_id=1, replica_groups=mesh['region'=16,'tile'=32] {'region','tile'}, use_global_device_ids=true, to_apply=%region_2.3 | all-reduce | flops 4160 | bytes 33280 | tf_op jit(solution)/shard_map/psum | solution.py:123
  200.9 120.4 %while.30 = (s32[]{:T(128)}, f32[64,64]{1,0:T(8,128)S(1)}, f32[64,64]{1,0:T(8,128)S(1)}, s32[]{:T(128)}, s32[]{:T(128)}) while((s32[]{:T(128)}, f32[64,64]{1,0:T(8,128)S(1)}, f32[64,64]{1,0:T(8,128)S(1)}, s32[]{:T(128)}, s32[]{:T(128)}) %tuple.90), condition=%wide.region_5.6_spmd.clone.clone, body=%wide.region_3.5_spmd.clone.clone.sunk | while | flops 168642 | bytes 84589 | solution.py:49
  201.1 0.8 fusion.173
  321.2 111.2 %while.29 = (s32[]{:T(128)}, f32[64,64]{1,0:T(8,128)S(1)}, f32[64,64]{1,0:T(8,128)S(1)}, s32[]{:T(128)}, s32[]{:T(128)}) while((s32[]{:T(128)}, f32[64,64]{1,0:T(8,128)S(1)}, f32[64,64]{1,0:T(8,128)S(1)}, s32[]{:T(128)}, s32[]{:T(128)}) %tuple.93), condition=%wide.region_8.9_spmd.clone, body=%wide.region_6.8_spmd.clone.sunk | while | flops 115330 | bytes 67164 | solution.py:63
  434.5 1.1 copy.76
  (726 shorter events, 201.2 us)
Async XLA Ops:
  0.0 30.1 %copy-start = (f32[64,4,4,128]{3,2,1,0:T(4,128)S(1)}, f32[64,4,4,128]{3,2,1,0:T(4,128)}, u32[]{:S(2)}) copy-start(f32[64,4,4,128]{3,2,1,0:T(4,128)} %param.12) | copy-start | bytes 1572868
  0.0 25.8 %copy-start.7 = (f32[64,4,128]{2,1,0:T(4,128)S(1)}, f32[64,4,128]{2,1,0:T(4,128)}, u32[]{:S(2)}) copy-start(f32[64,4,128]{2,1,0:T(4,128)} %param.13) | copy-start | bytes 393220
  10.1 15.7 %collective-permute-start = (f32[4,1,128]{2,1,0:T(1,128)S(1)}, f32[4,1,128]{2,1,0:T(1,128)S(1)}, u32[]{:S(2)}, u32[]{:S(2)}) collective-permute-start(f32[4,1,128]{2,1,0:T(1,128)S(1)} %get-tuple-element.244), channel_id=1, source_target_pairs={{0,32},{32,64},{64,96},{96,128},{128,160},{160,192},{192,224},{224... | collective-permute-start | bytes 6152 | tf_op jit(solution)/shard_map/ppermute | solution.py:18
  14.7 11.1 %collective-permute-start.1 = (f32[4,1,128]{2,1,0:T(1,128)S(1)}, f32[4,1,128]{2,1,0:T(1,128)S(1)}, u32[]{:S(2)}, u32[]{:S(2)}) collective-permute-start(f32[4,1,128]{2,1,0:T(1,128)S(1)} %get-tuple-element.245), channel_id=1, source_target_pairs={{32,0},{64,32},{96,64},{128,96},{160,128},{192,160},{224,192},{256... | collective-permute-start | bytes 6152 | tf_op jit(solution)/shard_map/ppermute | solution.py:21
  21.4 8.6 %collective-permute-start.4 = (f32[64,4,1,128]{3,0,2,1:T(8,128)S(1)}, f32[64,4,1,128]{3,0,2,1:T(8,128)S(1)}, u32[]{:S(2)}, u32[]{:S(2)}) collective-permute-start(f32[64,4,1,128]{3,0,2,1:T(8,128)S(1)} %get-tuple-element.241), channel_id=1, source_target_pairs={{0,32},{32,64},{64,96},{96,128},{128,160},{160,192},{192,224},{224... | collective-permute-start | bytes 393224 | tf_op jit(solution)/shard_map/ppermute | solution.py:18
  23.3 6.9 %collective-permute-start.5 = (f32[64,4,1,128]{3,0,2,1:T(8,128)S(1)}, f32[64,4,1,128]{3,0,2,1:T(8,128)S(1)}, u32[]{:S(2)}, u32[]{:S(2)}) collective-permute-start(f32[64,4,1,128]{3,0,2,1:T(8,128)S(1)} %get-tuple-element.240), channel_id=1, source_target_pairs={{32,0},{64,32},{96,64},{128,96},{160,128},{192,160},{224,192},{256... | collective-permute-start | bytes 393224 | tf_op jit(solution)/shard_map/ppermute | solution.py:21
  26.5 11.1 %collective-permute-start.2 = (f32[4,6,1]{2,1,0:T(8,128)}, f32[4,6,1]{2,1,0:T(8,128)}, u32[]{:S(2)}, u32[]{:S(2)}) collective-permute-start(f32[4,6,1]{2,1,0:T(8,128)} %get-tuple-element.242), channel_id=1, source_target_pairs={{0,1},{1,2},{2,3},{3,4},{4,5},{5,6},{6,7},{7,8},{8,9},{9,10},{10,1... | collective-permute-start | bytes 296 | tf_op jit(solution)/shard_map/ppermute | solution.py:18
  28.8 8.9 %collective-permute-start.3 = (f32[4,6,1]{2,1,0:T(8,128)}, f32[4,6,1]{2,1,0:T(8,128)}, u32[]{:S(2)}, u32[]{:S(2)}) collective-permute-start(f32[4,6,1]{2,1,0:T(8,128)} %get-tuple-element.243), channel_id=1, source_target_pairs={{1,0},{2,1},{3,2},{4,3},{5,4},{6,5},{7,6},{8,7},{9,8},{10,9},{11,1... | collective-permute-start | bytes 296 | tf_op jit(solution)/shard_map/ppermute | solution.py:21
  30.1 0.7 copy-start.3
  30.7 0.7 copy-start.5
  32.0 6.5 %collective-permute-start.6 = (f32[64,4,6,1]{0,1,3,2:T(4,128)S(1)}, f32[64,4,6,1]{0,1,3,2:T(4,128)S(1)}, u32[]{:S(2)}, u32[]{:S(2)}) collective-permute-start(f32[64,4,6,1]{0,1,3,2:T(4,128)S(1)} %copy.44), channel_id=1, source_target_pairs={{0,1},{1,2},{2,3},{3,4},{4,5},{5,6},{6,7},{7,8},{8,9},{9,10},{10,1... | collective-permute-start | bytes 18440 | tf_op jit(solution)/shard_map/ppermute | solution.py:18
  36.3 5.1 %collective-permute-start.7 = (f32[64,4,6,1]{0,1,3,2:T(4,128)S(1)}, f32[64,4,6,1]{0,1,3,2:T(4,128)S(1)}, u32[]{:S(2)}, u32[]{:S(2)}) collective-permute-start(f32[64,4,6,1]{0,1,3,2:T(4,128)S(1)} %copy.45), channel_id=1, source_target_pairs={{1,0},{2,1},{3,2},{4,3},{5,4},{6,5},{7,6},{8,7},{9,8},{10,9},{11,1... | collective-permute-start | bytes 18440 | tf_op jit(solution)/shard_map/ppermute | solution.py:21
  38.5 4.0 copy-start.1
  42.5 0.9 copy-start.4
  42.5 1.0 copy-start.6
  44.5 7.0 %collective-permute-start.8 = (f32[64,4,1,128]{3,0,2,1:T(8,128)S(1)}, f32[64,4,1,128]{3,0,2,1:T(8,128)S(1)}, u32[]{:S(2)}, u32[]{:S(2)}) collective-permute-start(f32[64,4,1,128]{3,0,2,1:T(8,128)S(1)} %get-tuple-element.238), channel_id=1, source_target_pairs={{0,32},{32,64},{64,96},{96,128},{128,160},{160,192},{192,224},{224... | collective-permute-start | bytes 393224 | tf_op jit(solution)/shard_map/ppermute | solution.py:18
  49.6 6.3 %collective-permute-start.9 = (f32[64,4,1,128]{3,0,2,1:T(8,128)S(1)}, f32[64,4,1,128]{3,0,2,1:T(8,128)S(1)}, u32[]{:S(2)}, u32[]{:S(2)}) collective-permute-start(f32[64,4,1,128]{3,0,2,1:T(8,128)S(1)} %get-tuple-element.239), channel_id=1, source_target_pairs={{32,0},{64,32},{96,64},{128,96},{160,128},{192,160},{224,192},{256... | collective-permute-start | bytes 393224 | tf_op jit(solution)/shard_map/ppermute | solution.py:21
  56.3 7.1 %copy-start.8 = (s32[256]{0:T(256)S(1)}, s32[256]{0:T(256)}, u32[]{:S(2)}) copy-start(s32[256]{0:T(256)} %param.16) | copy-start | bytes 3076
  56.3 12.1 %copy-start.2 = (f32[4,6,130]{2,1,0:T(8,128)S(1)}, f32[4,6,130]{2,1,0:T(8,128)}, u32[]{:S(2)}) copy-start(f32[4,6,130]{2,1,0:T(8,128)} %copy-done.1) | copy-start | bytes 37444
  56.6 6.8 %collective-permute-start.10 = (f32[64,4,6,1]{0,1,3,2:T(4,128)S(1)}, f32[64,4,6,1]{0,1,3,2:T(4,128)S(1)}, u32[]{:S(2)}, u32[]{:S(2)}) collective-permute-start(f32[64,4,6,1]{0,1,3,2:T(4,128)S(1)} %copy.60), channel_id=1, source_target_pairs={{0,1},{1,2},{2,3},{3,4},{4,5},{5,6},{6,7},{7,8},{8,9},{9,10},{10,1... | collective-permute-start | bytes 18440 | tf_op jit(solution)/shard_map/ppermute | solution.py:18
  62.1 5.9 %collective-permute-start.11 = (f32[64,4,6,1]{0,1,3,2:T(4,128)S(1)}, f32[64,4,6,1]{0,1,3,2:T(4,128)S(1)}, u32[]{:S(2)}, u32[]{:S(2)}) collective-permute-start(f32[64,4,6,1]{0,1,3,2:T(4,128)S(1)} %copy.61), channel_id=1, source_target_pairs={{1,0},{2,1},{3,2},{4,3},{5,4},{6,5},{7,6},{8,7},{9,8},{10,9},{11,1... | collective-permute-start | bytes 18440 | tf_op jit(solution)/shard_map/ppermute | solution.py:21
  70.4 4.9 %collective-permute-start.12 = (f32[64,4,1,128]{3,0,2,1:T(8,128)S(1)}, f32[64,4,1,128]{3,0,2,1:T(8,128)S(1)}, u32[]{:S(2)}, u32[]{:S(2)}) collective-permute-start(f32[64,4,1,128]{3,0,2,1:T(8,128)S(1)} %get-tuple-element.236), channel_id=1, source_target_pairs={{0,32},{32,64},{64,96},{96,128},{128,160},{160,192},{192,224},{224... | collective-permute-start | bytes 393224 | tf_op jit(solution)/shard_map/ppermute | solution.py:18
  73.4 6.3 %collective-permute-start.13 = (f32[64,4,1,128]{3,0,2,1:T(8,128)S(1)}, f32[64,4,1,128]{3,0,2,1:T(8,128)S(1)}, u32[]{:S(2)}, u32[]{:S(2)}) collective-permute-start(f32[64,4,1,128]{3,0,2,1:T(8,128)S(1)} %get-tuple-element.237), channel_id=1, source_target_pairs={{32,0},{64,32},{96,64},{128,96},{160,128},{192,160},{224,192},{256... | collective-permute-start | bytes 393224 | tf_op jit(solution)/shard_map/ppermute | solution.py:21
  80.3 7.1 %collective-permute-start.14 = (f32[64,4,6,1]{0,1,3,2:T(4,128)S(1)}, f32[64,4,6,1]{0,1,3,2:T(4,128)S(1)}, u32[]{:S(2)}, u32[]{:S(2)}) collective-permute-start(f32[64,4,6,1]{0,1,3,2:T(4,128)S(1)} %copy.66), channel_id=1, source_target_pairs={{0,1},{1,2},{2,3},{3,4},{4,5},{5,6},{6,7},{7,8},{8,9},{9,10},{10,1... | collective-permute-start | bytes 18440 | tf_op jit(solution)/shard_map/ppermute | solution.py:18
  85.5 4.7 %collective-permute-start.15 = (f32[64,4,6,1]{0,1,3,2:T(4,128)S(1)}, f32[64,4,6,1]{0,1,3,2:T(4,128)S(1)}, u32[]{:S(2)}, u32[]{:S(2)}) collective-permute-start(f32[64,4,6,1]{0,1,3,2:T(4,128)S(1)} %copy.67), channel_id=1, source_target_pairs={{1,0},{2,1},{3,2},{4,3},{5,4},{6,5},{7,6},{8,7},{9,8},{10,9},{11,1... | collective-permute-start | bytes 18440 | tf_op jit(solution)/shard_map/ppermute | solution.py:21
  92.6 1.3 copy-start.9
  92.6 1.3 copy-start.10
where the time goes:
time: 441 us; the launch traced here: 436 us
  matrix products  178 us (40%)
  blocking collectives  106 us (24%)
  starting transfers between devices  47.8 us (11%)
  loops' own time  45.1 us (10%)
  other arithmetic  26.4 us (6%)
  waiting for transfers between devices  18 us (4%)
  local copies, waits for them, and re-layouts  13.4 us (3%)
    psum x1, blocking collectives, shards(): gram, bvec = lax.psum((gram, bvec), ('region', 'tile'))  106 us
    dot_general x64, matrix products, column_step(): jnp.dot(lower, row_now, precision=lax.Precision.HIGHEST)  53.6 us
    dot_general x64, matrix products, row_step(): row_now = jnp.dot(onehot, lower, precision=lax.Precision.HIGHEST)  52.8 us
    dot_general x64, matrix products, row_step(): jnp.dot(row_now, solved, precision=lax.Precision.HIGHEST)  52.7 us
    another operation x1, loops' own time, cholesky_lower(): return lax.fori_loop(0, order, column_step, jnp.zeros_like(matrix))  44.6 us
    ppermute x8, starting transfers between devices, extended(): lax.ppermute(lax.slice_in_dim(block, block.shape[dim] - width, None, axis...  30.9 us
    ppermute x8, waiting for transfers between devices, extended(): lax.ppermute(lax.slice_in_dim(block, 0, width, axis=dim), axis, backward)  17.9 us
    ppermute x8, starting transfers between devices, extended(): lax.ppermute(lax.slice_in_dim(block, 0, width, axis=dim), axis, backward)  16.9 us
  transfers between devices with their start and end apart: 16, of which 5 were waited for; matrix products, arithmetic and copies ran while one was open for 1% of the time, Pallas kernels for 0%

commit v1 on v0

v1 whole, which is shorter than its diff:
```python
import functools

import jax
import jax.numpy as jnp
from jax import lax
from jax.experimental import pallas as pl
from jax.experimental.pallas import tpu as pltpu
from jax.sharding import PartitionSpec as P

STEPS = 3
MEM = 64
LEV = 4
ROWS = 4
COLS = 128
GROUPS = MEM // 8
CELLS = LEV * ROWS
HALO = 3
EXT = ROWS + 2 * HALO
PAD = 72
MSG_FORCE = LEV * HALO * MEM
MSG_KC = MSG_FORCE + 2 * MEM
MSG_EDGE = MSG_KC + CELLS
MSG_ROWS = MSG_EDGE + PAD
PAYLOAD = 20
HIGHEST = lax.Precision.HIGHEST
F32 = jnp.float32


def roll(x, shift):
    shift = shift % COLS
    return x if shift == 0 else pltpu.roll(x, shift, 1)


def lanes(rows=8):
    return lax.broadcasted_iota(jnp.int32, (rows, COLS), 1)


def edge_pack(rows_of):
    lane = lanes()
    out = jnp.zeros((8, COLS), F32)
    for l in range(LEV + 1):
        for r in range(ROWS):
            block = rows_of(l, r)
            if block is None:
                continue
            start = l * 24 + r * 6
            out = jnp.where((lane >= start) & (lane < start + 6), roll(block, 3 + start), out)
    return out


def pack_kernel(h_ref, f_ref, cls_ref, k_ref, up_ref, dn_ref, edge_ref, kc_ref):
    cls = cls_ref[...]
    kc = jnp.zeros(cls.shape, F32)
    for index in range(12):
        kc = jnp.where(cls == index, k_ref[index], kc)
    kc_ref[...] = kc
    up_ref[pl.ds(MSG_KC, CELLS), :] = kc
    dn_ref[pl.ds(MSG_KC, CELLS), :] = kc
    kedge = edge_pack(
        lambda l, r: None
        if l == LEV
        else jnp.broadcast_to(kc[l * ROWS + r : l * ROWS + r + 1, :], (8, COLS))
    )
    edge_ref[pl.ds(MEM, 8), :] = kedge
    up_ref[pl.ds(MSG_EDGE + MEM, 8), :] = kedge
    dn_ref[pl.ds(MSG_EDGE + MEM, 8), :] = kedge

    for g in range(GROUPS):
        h = {}
        for l in range(LEV):
            for r in range(ROWS):
                block = h_ref[pl.ds(g * 8 * CELLS + l * ROWS + r, 8, stride=CELLS), :]
                h[l, r] = block
                if r < HALO:
                    up_ref[pl.ds((l * HALO + r) * MEM + g * 8, 8), :] = block
                if r >= ROWS - HALO:
                    dn_ref[pl.ds((l * HALO + r - 1) * MEM + g * 8, 8), :] = block
        for r in range(ROWS):
            block = f_ref[pl.ds(g * 8 * ROWS + r, 8, stride=ROWS), :]
            h[LEV, r] = block
            if r < 2:
                up_ref[pl.ds(MSG_FORCE + r * MEM + g * 8, 8), :] = block
            else:
                dn_ref[pl.ds(MSG_FORCE + (r - 2) * MEM + g * 8, 8), :] = block
        edge = edge_pack(lambda l, r: h[l, r])
        edge_ref[pl.ds(g * 8, 8), :] = edge
        up_ref[pl.ds(MSG_EDGE + g * 8, 8), :] = edge
        dn_ref[pl.ds(MSG_EDGE + g * 8, 8), :] = edge


def obs_kernel(idx_ref, val_ref, var_ref, cnt_ref, out_ref):
    slots = idx_ref.shape[1]
    idx = idx_ref[...]
    slot = lax.broadcasted_iota(jnp.int32, (1, slots), 1)
    weight = jnp.where(slot < cnt_ref[0], 1.0 / var_ref[...], 0.0)
    high = idx // COLS
    low = idx % COLS
    place = lax.broadcasted_iota(jnp.int32, (CELLS, slots), 0) == high
    lhs = jnp.concatenate(
        [jnp.where(place, weight, 0.0), jnp.where(place, weight * val_ref[...], 0.0)], axis=0
    )
    rhs = jnp.where(lax.broadcasted_iota(jnp.int32, (COLS, slots), 0) == low, 1.0, 0.0)
    out_ref[...] = lax.dot_general(
        lhs, rhs, (((1,), (1,)), ((), ())), precision=HIGHEST, preferred_element_type=F32
    )


def forecast_kernel(
    regions, tiles,
    h_ref, f_ref, kc_ref, obs_ref, above_ref, below_ref, edge_ref, el_ref, er_ref,
    uel_ref, uer_ref, del_ref, der_ref,
    dev_ref, mean_ref, pay_ref,
    z_ref, sum_ref, ks_ref, gram_ref,
):
    ri = lax.axis_index("region")
    ti = lax.axis_index("tile")
    top_ok = jnp.where(ri > 0, 1.0, 0.0)
    bot_ok = jnp.where(ri < regions - 1, 1.0, 0.0)
    left_ok = jnp.where(ti > 0, 1.0, 0.0)
    right_ok = jnp.where(ti < tiles - 1, 1.0, 0.0)
    lane = lanes()
    half = lane % 64
    srow = half // 6
    scol = half % 6
    is_left = lane < 64
    row_ok = jnp.where(srow < HALO, top_ok, jnp.where(srow >= HALO + ROWS, bot_ok, 1.0))
    side_ok = jnp.where(
        is_left, jnp.where(scol < 3, left_ok, 1.0), jnp.where(scol >= 3, right_ok, 1.0)
    )
    smask = jnp.where(half < 60, row_ok * side_ok, 0.0)
    low_k = lane % 6 < 3

    def strips(base):
        own, left, right = base(edge_ref, 0), base(el_ref, 0), base(er_ref, 0)
        uown, ul, ur = base(above_ref, MSG_EDGE), base(uel_ref, 0), base(uer_ref, 0)
        down, dl, dr = base(below_ref, MSG_EDGE), base(del_ref, 0), base(der_ref, 0)
        parts = (
            (jnp.where(low_k, ul, uown), jnp.where(low_k, uown, ur), -1),
            (jnp.where(low_k, left, own), jnp.where(low_k, own, right), 3),
            (jnp.where(low_k, dl, down), jnp.where(low_k, down, dr), 7),
        )
        out = []
        for l in range(LEV + 1):
            strip = jnp.zeros((8, COLS), F32)
            for lo, hi, first in parts:
                inside = (srow >= first) & (srow < first + ROWS)
                strip = jnp.where(inside & is_left, roll(lo, first * 6 - l * 24), strip)
                strip = jnp.where(inside & ~is_left, roll(hi, 64 + first * 6 - l * 24), strip)
            out.append(strip * smask)
        return out

    kstrip = strips(lambda ref, base: ref[pl.ds(base + MEM, 8), :])
    for l in range(LEV):
        ks_ref[pl.ds(l * 8, 8), :] = kstrip[l]
    sum_ref[...] = jnp.zeros(sum_ref.shape, F32)

    def kc_row(l, e):
        r = e - HALO
        if r < 0:
            at = MSG_KC + l * ROWS + r + ROWS
            return above_ref[at : at + 1, :] * top_ok
        if r >= ROWS:
            at = MSG_KC + l * ROWS + r - ROWS
            return below_ref[at : at + 1, :] * bot_ok
        at = l * ROWS + r
        return kc_ref[at : at + 1, :]

    kcs = {(l, e): kc_row(l, e) for l in range(LEV) for e in range(EXT)}

    def conduct(kc, h):
        return kc + (0.5 * kc) * jnp.tanh(0.5 * h)

    def group(g, carry):
        base = g * 8
        hs = strips(lambda ref, first: ref[pl.ds(first + base, 8), :])
        fs = hs[LEV]
        h = {}
        force = {}
        for l in range(LEV):
            for e in range(EXT):
                r = e - HALO
                if r < 0:
                    at = (l * HALO + r + HALO) * MEM
                    h[l, e] = above_ref[pl.ds(at + base, 8), :] * top_ok
                elif r >= ROWS:
                    at = (l * HALO + r - ROWS) * MEM
                    h[l, e] = below_ref[pl.ds(at + base, 8), :] * bot_ok
                else:
                    h[l, e] = h_ref[pl.ds(g * (8 * CELLS) + l * ROWS + r, 8, stride=CELLS), :]
        for e in range(1, EXT - 1):
            r = e - HALO
            if r < 0:
                force[e] = above_ref[pl.ds(MSG_FORCE + (r + 2) * MEM + base, 8), :]
            elif r >= ROWS:
                force[e] = below_ref[pl.ds(MSG_FORCE + (r - ROWS) * MEM + base, 8), :]
            else:
                force[e] = f_ref[pl.ds(g * (8 * ROWS) + r, 8, stride=ROWS), :]

        for step in range(STEPS):
            faces = []
            sk = [conduct(ks_ref[pl.ds(l * 8, 8), :], hs[l]) for l in range(LEV)]
            for l in range(LEV):
                faces.append((sk[l] + roll(sk[l], -1)) * (roll(hs[l], -1) - hs[l]))
            if step < STEPS - 1:
                vert = [
                    0.5 * (sk[l] + sk[l + 1]) * (hs[l + 1] - hs[l]) for l in range(LEV - 1)
                ]
                fresh = []
                for l in range(LEV):
                    down = (sk[l] + roll(sk[l], -6)) * (roll(hs[l], -6) - hs[l])
                    flux = faces[l] - roll(faces[l], 1) + down - roll(down, 6)
                    if l < LEV - 1:
                        flux = flux + vert[l]
                    if l > 0:
                        flux = flux - vert[l - 1]
                    flux = 0.125 * flux
                    if l == 0:
                        flux = flux + 0.25 * fs
                    fresh.append((hs[l] + flux) * smask)
                hs = fresh + [fs]
            k = {
                (l, e): conduct(kcs[l, e], h[l, e])
                for l in range(LEV)
                for e in range(step, EXT - step)
            }
            new = {}
            rowface = {}
            for e in range(step, EXT - step):
                above_vert = None
                for l in range(LEV):
                    if e < EXT - step - 1:
                        rowface[l, e] = (k[l, e] + k[l, e + 1]) * (h[l, e + 1] - h[l, e])
                    if e == step or e == EXT - step - 1:
                        continue
                    here, kh = h[l, e], k[l, e]
                    face = (kh + roll(kh, -1)) * (roll(here, -1) - here)
                    face = jnp.where(lane == COLS - 1, roll(faces[l], 61 - e * 6), face)
                    behind = jnp.where(lane == 0, roll(faces[l], -(e * 6 + 2)), roll(face, 1))
                    flux = (face - behind) + (rowface[l, e] - rowface[l, e - 1])
                    if l < LEV - 1:
                        vert = 0.5 * (kh + k[l + 1, e]) * (h[l + 1, e] - here)
                        flux = flux + vert
                    if l > 0:
                        flux = flux - above_vert
                    if l < LEV - 1:
                        above_vert = vert
                    flux = 0.125 * flux
                    if l == 0:
                        flux = flux + 0.25 * force[e]
                    value = here + flux
                    if e < HALO:
                        value = value * top_ok
                    elif e >= HALO + ROWS:
                        value = value * bot_ok
                    new[l, e] = value
            h = new
        for l in range(LEV):
            for r in range(ROWS):
                lr = l * ROWS + r
                value = h[l, r + HALO]
                dev_ref[pl.ds(base, 8), lr * COLS : (lr + 1) * COLS] = value
                sum_ref[lr * 8 : lr * 8 + 8, :] += value
        return carry

    lax.fori_loop(0, GROUPS, group, 0)

    for lr in range(CELLS):
        mean = jnp.sum(sum_ref[lr * 8 : lr * 8 + 8, :], axis=0, keepdims=True) * (1.0 / MEM)
        mean_ref[lr : lr + 1, :] = mean
        cols = slice(lr * COLS, (lr + 1) * COLS)
        dev = dev_ref[:, cols] - mean
        dev_ref[:, cols] = dev
        scale = obs_ref[lr : lr + 1, :]
        z_ref[0:MEM, cols] = dev * scale
        rest = obs_ref[CELLS + lr : CELLS + lr + 1, :] - scale * mean
        z_ref[MEM : MEM + 8, cols] = jnp.broadcast_to(rest, (8, COLS))
    gram_ref[:, 0:MEM] = lax.dot_general(
        z_ref[...], dev_ref[...], (((1,), (1,)), ((), ())),
        precision=HIGHEST, preferred_element_type=F32,
    )
    gram_ref[:, MEM:COLS] = jnp.zeros((PAD, COLS - MEM), F32)

    def stripe(i):
        return gram_ref[8 * i : 8 * i + 8, :]

    def joined(i):
        if i == 0:
            return stripe(0)
        other = stripe(8 - i)
        return jnp.where(lane >= 8 * i, stripe(i), roll(other, 8 * i - MEM))

    vec = stripe(8)
    sub = lax.broadcasted_iota(jnp.int32, (8, COLS), 0)
    part = jnp.where(sub % 2 == 0, vec, roll(vec, -32))
    last = jnp.where(lane >= 32, stripe(4), part)
    first = jnp.where(lane < MEM, joined(0), roll(joined(1), MEM))
    second = jnp.where(lane < MEM, joined(2), roll(joined(3), MEM))
    third = jnp.where(
        lane[0:4] < MEM, last[0:4], roll(last[4:8], MEM)
    )
    for c in range(regions):
        pay_ref[c, 0:8, :] = first
        pay_ref[c, 8:16, :] = second
        pay_ref[c, 16:20, :] = third


def analysis_kernel(copies, pay_ref, dev_ref, mean_ref, out_ref, m_ref):
    lane = lanes()
    sub = lax.broadcasted_iota(jnp.int32, (8, COLS), 0)
    first = pay_ref[0, 0:8, :]
    second = pay_ref[0, 8:16, :]
    third = pay_ref[0, 16:20, :]
    for c in range(1, copies):
        first = first + pay_ref[c, 0:8, :]
        second = second + pay_ref[c, 8:16, :]
        third = third + pay_ref[c, 16:20, :]
    halves = [
        first,
        roll(first, MEM),
        second,
        roll(second, MEM),
        jnp.concatenate([third, roll(third, MEM)], axis=0),
    ]
    for i in range(8):
        block = halves[i] if i <= 4 else roll(halves[8 - i], MEM - 8 * (8 - i))
        keep = (lane >= 8 * i) & (lane < MEM)
        block = jnp.where(keep, block, 0.0)
        block = block + jnp.where(lane == sub + 8 * i, MEM - 1.0, 0.0)
        block = block + jnp.where(lane == sub + (8 * i + MEM), 1.0, 0.0)
        m_ref[8 * i : 8 * i + 8, :] = block
    tail = halves[4]
    bvec = jnp.where(
        lane[0:1] < MEM + 32, roll(tail[0:1, :], MEM), roll(tail[1:2, :], MEM + 32)
    )

    for kb in range(8):
        block = m_ref[8 * kb : 8 * kb + 8, :]
        for j in range(8):
            at = 8 * kb + j
            inv = lax.rsqrt(block[j : j + 1, at : at + 1])
            prow = block[j : j + 1, :] * inv
            factor = block[:, at : at + 1] * inv
            block = jnp.where(
                sub > j, block - factor * prow, jnp.where(sub == j, prow, block)
            )
        m_ref[8 * kb : 8 * kb + 8, :] = block
        if kb < 7:
            later = 8 * (kb + 1)
            update = lax.dot_general(
                block[:, 0:MEM], block, (((0,), (0,)), ((), ())),
                precision=HIGHEST, preferred_element_type=F32,
            )
            m_ref[later:MEM, :] = m_ref[later:MEM, :] - update[later:MEM, :]

    inverse = m_ref[...]
    bvec = jnp.where(lane[0:1] >= MEM, bvec, 0.0)
    y = jnp.sum(inverse * bvec, axis=1, keepdims=True)
    w = jnp.sum(inverse * y, axis=0, keepdims=True)
    blend = (inverse * jnp.sqrt(jnp.full((1, COLS), MEM - 1.0, F32)) + w)[:, MEM:COLS]
    for lr in range(CELLS):
        cols = slice(lr * COLS, (lr + 1) * COLS)
        value = mean_ref[lr : lr + 1, :] + jnp.dot(
            blend, dev_ref[:, cols], precision=HIGHEST, preferred_element_type=F32
        )
        out_ref[pl.ds(lr, MEM, stride=CELLS), :] = value


def vmem():
    return pl.BlockSpec(memory_space=pltpu.VMEM)


def smem():
    return pl.BlockSpec(memory_space=pltpu.SMEM)


PARAMS = pltpu.CompilerParams(vmem_limit_bytes=32 * 1024 * 1024)


def shift(x, axis, by):
    count = lax.axis_size(axis)
    return lax.ppermute(x, axis, [(i, (i + by) % count) for i in range(count)])


def shards(prior, source, soil_class, soil_k, obs_index, obs_value, obs_var, obs_count):
    regions, tiles = lax.axis_size("region"), lax.axis_size("tile")
    prior = prior.reshape(MEM * CELLS, COLS)
    source = source.reshape(MEM * ROWS, COLS)
    soil_class = soil_class.reshape(CELLS, COLS)
    slots = obs_index.shape[0]

    def out(*shape):
        return jax.ShapeDtypeStruct(shape, F32)

    up, dn, edge, kc = pl.pallas_call(
        pack_kernel,
        out_shape=(out(MSG_ROWS, COLS), out(MSG_ROWS, COLS), out(PAD, COLS), out(CELLS, COLS)),
        in_specs=[vmem(), vmem(), vmem(), smem()],
        out_specs=(vmem(),) * 4,
        compiler_params=PARAMS,
        name="pack",
    )(prior, source, soil_class, soil_k)
    above = shift(dn, "region", 1)
    below = shift(up, "region", -1)
    el = shift(edge, "tile", 1)
    er = shift(edge, "tile", -1)
    uel, uer = shift(el, "region", 1), shift(er, "region", 1)
    bel, ber = shift(el, "region", -1), shift(er, "region", -1)
    obs = pl.pallas_call(
        obs_kernel,
        out_shape=out(2 * CELLS, COLS),
        in_specs=[vmem(), vmem(), vmem(), smem()],
        out_specs=vmem(),
        compiler_params=PARAMS,
        name="scatter_obs",
    )(
        obs_index.reshape(1, slots), obs_value.reshape(1, slots), obs_var.reshape(1, slots),
        obs_count,
    )
    dev, mean, pay = pl.pallas_call(
        functools.partial(forecast_kernel, regions, tiles),
        out_shape=(out(MEM, CELLS * COLS), out(CELLS, COLS), out(regions, PAYLOAD, COLS)),
        in_specs=[vmem()] * 13,
        out_specs=(vmem(),) * 3,
        scratch_shapes=[
            pltpu.VMEM((PAD, CELLS * COLS), F32),
            pltpu.VMEM((CELLS * 8, COLS), F32),
            pltpu.VMEM((LEV * 8, COLS), F32),
            pltpu.VMEM((PAD, COLS), F32),
        ],
        compiler_params=PARAMS,
        name="forecast",
    )(prior, source, kc, obs, above, below, edge, el, er, uel, uer, bel, ber)
    part = lax.all_to_all(pay, "region", 0, 0).sum(axis=0)
    pay = lax.all_to_all(jnp.broadcast_to(part, (tiles,) + part.shape), "tile", 0, 0)
    result = pl.pallas_call(
        functools.partial(analysis_kernel, tiles),
        out_shape=out(MEM * CELLS, COLS),
        in_specs=[vmem()] * 3,
        out_specs=vmem(),
        scratch_shapes=[pltpu.VMEM((MEM, COLS), F32)],
        compiler_params=PARAMS,
        name="analysis",
    )(pay, dev, mean)
    return result.reshape(MEM, LEV, ROWS, COLS)


def solution(mesh):
    return jax.shard_map(
        shards,
        mesh=mesh,
        in_specs=(
            P(None, None, "region", "tile"),
            P(None, "region", "tile"),
            P(None, "region", "tile"),
            P(),
            P(("region", "tile")),
            P(("region", "tile")),
            P(("region", "tile")),
            P(("region", "tile")),
        ),
        out_specs=P(None, None, "region", "tile"),
        check_vma=False,
    )
```

time: 441 us -> 86.6 us (0.20); the launches traced: 436 us -> 86.3 us
  matrix products: 178 us -> 0 us
  blocking collectives: 106 us -> 37.5 us
  loops' own time: 45.1 us -> 0 us
  other arithmetic: 26.4 us -> 0.02 us
  starting transfers between devices: 47.8 us -> 22.9 us
  Pallas kernels: 0 us -> 17.1 us
  waiting for transfers between devices: 18 us -> 4.06 us
  local copies, waits for them, and re-layouts: 13.4 us -> 3.99 us
    dot_general x325 -> x0, matrix products: 178 us -> none  [the longest x64 53.6 us: column_step(): jnp.dot(lower, row_now, precision=lax.Precision.HIGHEST)]
    psum x1 -> x0, blocking collectives: 106 us -> none  [shards(): gram, bvec = lax.psum((gram, bvec), ('region', 'tile'))]
    another operation x2 -> x0, loops' own time: 45.1 us -> none  [the longest x1 44.6 us: cholesky_lower(): return lax.fori_loop(0, order, column_step, jnp.zeros_like(matrix))]
    all_to_all x0 -> x2, blocking collectives: none -> 37.5 us  [the longest x1 20.2 us: shards(): part = lax.all_to_all(pay, 'region', 0, 0).sum(axis=0)]
    ppermute x16 -> x8, starting transfers between devices: 47.8 us -> 22.9 us  [shift(): return lax.ppermute(x, axis, [(i, (i + by) % count) for i in range(count)])]
    add x132 -> x0, other arithmetic: 20.3 us -> none  [the longest x1 8.26 us: lookup(): total = total + jnp.where(soil_class == index, soil_k[index], 0.0)]
    pallas_call x0 -> x4, Pallas kernels: none -> 17.1 us  [the longest x1 8.23 us: shards(): pl.pallas_call(functools.partial(analysis_kernel, tiles), out_shape=out(M...]
    ppermute x16 -> x8, waiting for transfers between devices: 18 us -> 4.06 us  [shift(): return lax.ppermute(x, axis, [(i, (i + by) % count) for i in range(count)])]
  transfers between devices with their start and end apart: 16 -> 8, of which waited for: 5 -> 1; matrix products, arithmetic and copies ran while one was open for 1% -> 0% of each run, Pallas kernels for 0% -> 0%
where the time goes in v1:
time: 86.6 us; the launch traced here: 86.3 us
  blocking collectives  37.5 us (43%)
  starting transfers between devices  22.9 us (26%)
  Pallas kernels  17.1 us (20%)
  waiting for transfers between devices  4.06 us (5%)
  local copies, waits for them, and re-layouts  3.99 us (5%)
    ppermute x8, starting transfers between devices, shift(): return lax.ppermute(x, axis, [(i, (i + by) % count) for i in range(count)])  22.9 us
    all_to_all x1, blocking collectives, shards(): part = lax.all_to_all(pay, 'region', 0, 0).sum(axis=0)  20.2 us
    all_to_all x1, blocking collectives, shards(): lax.all_to_all(jnp.broadcast_to(part, (tiles,) + part.shape), 'tile', 0, 0)  17.3 us
    pallas_call x1, Pallas kernels, shards(): pl.pallas_call(functools.partial(analysis_kernel, tiles), out_shape=out(M...  8.23 us
    pallas_call x1, Pallas kernels, shards(): pl.pallas_call(functools.partial(forecast_kernel, regions, tiles), out_sh...  7.78 us
    ppermute x8, waiting for transfers between devices, shift(): return lax.ppermute(x, axis, [(i, (i + by) % count) for i in range(count)])  4.06 us
    unnamed x16, local copies, waits for them, and re-layouts  3.96 us
  transfers between devices with their start and end apart: 8, of which 1 were waited for; matrix products, arithmetic and copies ran while one was open for 0% of the time, Pallas kernels for 0%

profile of v1, /device:TPU:1, one launch (start us, length us, event | category | flops | bytes accessed | tf_op | source)
XLA Modules:
  0.0 86.3 jit_solution(15275331194684922224)
XLA Ops:
  0.0 0.0 copy-start.7
  0.0 0.7 copy-done.7
  0.7 1.0 %copy-done = f32[64,4,4,128]{3,2,1,0:T(4,128)S(1)} copy-done((f32[64,4,4,128]{3,2,1,0:T(4,128)S(1)}, f32[64,4,4,128]{3,2,1,0:T(4,128)}, u32[]{:S(2)}) %copy-start) | copy-done | bytes 524312
  1.7 0.9 %copy-done.2 = f32[64,4,128]{2,1,0:T(4,128)S(1)} copy-done((f32[64,4,128]{2,1,0:T(4,128)S(1)}, f32[64,4,128]{2,1,0:T(4,128)}, u32[]{:S(2)}) %copy-start.2) | copy-done | bytes 131096
  2.6 0.7 copy-done.3
  3.3 0.8 pack.1
  4.1 2.7 %collective-permute-start = (f32[984,128]{1,0:T(8,128)S(1)}, f32[984,128]{1,0:T(8,128)S(1)}, u32[]{:S(2)}, u32[]{:S(2)}) collective-permute-start(f32[984,128]{1,0:T(8,128)S(1)} %get-tuple-element.13), channel_id=1, source_target_pairs={{0,32},{32,64},{64,96},{96,128},{128,160},{160,192},{192,224},{224... | collective-permute-start | bytes 1511432 | tf_op jit(solution)/shard_map/ppermute | solution.py:381
  6.8 4.2 %collective-permute-start.1 = (f32[984,128]{1,0:T(8,128)S(1)}, f32[984,128]{1,0:T(8,128)S(1)}, u32[]{:S(2)}, u32[]{:S(2)}) collective-permute-start(f32[984,128]{1,0:T(8,128)S(1)} %get-tuple-element.14), channel_id=1, source_target_pairs={{0,480},{32,0},{64,32},{96,64},{128,96},{160,128},{192,160},{224,1... | collective-permute-start | bytes 1511432 | tf_op jit(solution)/shard_map/ppermute | solution.py:381
  11.1 8.8 %collective-permute-start.3 = (f32[72,128]{1,0:T(8,128)S(1)}, f32[72,128]{1,0:T(8,128)S(1)}, u32[]{:S(2)}, u32[]{:S(2)}) collective-permute-start(f32[72,128]{1,0:T(8,128)S(1)} %get-tuple-element.15.edge_ref), channel_id=1, source_target_pairs={{0,31},{1,0},{2,1},{3,2},{4,3},{5,4},{6,5},{7,6},{8,7},{9,8},{10,9... | collective-permute-start | bytes 110600 | tf_op jit(solution)/shard_map/ppermute | solution.py:381
  19.8 1.9 %collective-permute-start.2 = (f32[72,128]{1,0:T(8,128)S(1)}, f32[72,128]{1,0:T(8,128)S(1)}, u32[]{:S(2)}, u32[]{:S(2)}) collective-permute-start(f32[72,128]{1,0:T(8,128)S(1)} %get-tuple-element.15.edge_ref), channel_id=1, source_target_pairs={{0,1},{1,2},{2,3},{3,4},{4,5},{5,6},{6,7},{7,8},{8,9},{9,10},{10,1... | collective-permute-start | bytes 110600 | tf_op jit(solution)/shard_map/ppermute | solution.py:381
  21.8 0.0 collective-permute-done.3.er_ref
  21.8 2.1 %collective-permute-start.7 = (f32[72,128]{1,0:T(8,128)S(1)}, f32[72,128]{1,0:T(8,128)S(1)}, u32[]{:S(2)}, u32[]{:S(2)}) collective-permute-start(f32[72,128]{1,0:T(8,128)S(1)} %collective-permute-done.3.er_ref), channel_id=1, source_target_pairs={{0,480},{32,0},{64,32},{96,64},{128,96},{160,128},{192,160},{224,1... | collective-permute-start | bytes 110600 | tf_op jit(solution)/shard_map/ppermute | solution.py:381
  23.8 0.0 collective-permute-start.5
  23.8 4.0 %collective-permute-done.2.el_ref = f32[72,128]{1,0:T(8,128)S(1)} collective-permute-done((f32[72,128]{1,0:T(8,128)S(1)}, f32[72,128]{1,0:T(8,128)S(1)}, u32[]{:S(2)}, u32[]{:S(2)}) %collective-permute-start.2) | collective-permute-done | bytes 36896 | tf_op jit(solution)/shard_map/ppermute | solution.py:381
  27.9 3.2 %collective-permute-start.6 = (f32[72,128]{1,0:T(8,128)S(1)}, f32[72,128]{1,0:T(8,128)S(1)}, u32[]{:S(2)}, u32[]{:S(2)}) collective-permute-start(f32[72,128]{1,0:T(8,128)S(1)} %collective-permute-done.2.el_ref), channel_id=1, source_target_pairs={{0,480},{32,0},{64,32},{96,64},{128,96},{160,128},{192,160},{224,1... | collective-permute-start | bytes 110600 | tf_op jit(solution)/shard_map/ppermute | solution.py:381
  31.1 0.0 collective-permute-done.7.der_ref
  31.1 0.0 collective-permute-start.4
  31.7 0.0 copy-start.4
  31.7 0.0 copy-done.5
  31.7 0.0 copy-done.6
  31.7 0.7 copy-done.4
  32.4 0.2 scatter_obs.1.obs_ref
  32.6 0.0 collective-permute-done.5.uer_ref
  32.6 0.0 collective-permute-done.6.del_ref
  32.7 0.0 collective-permute-done.4.uel_ref
  32.7 0.0 collective-permute-done.above_ref
  32.7 0.0 collective-permute-done.1.below_ref
  32.7 0.0 copy-done.1
  32.7 7.8 %forecast.1 = (f32[64,2048]{1,0:T(8,128)S(1)}, f32[16,128]{1,0:T(8,128)S(1)}, f32[16,20,128]{2,1,0:T(8,128)S(1)}) custom-call(f32[1024,128]{1,0:T(8,128)S(1)} %bitcast.8, f32[256,128]{1,0:T(8,128)S(1)} %bitcast.10, f32[16,128]{1,0:T(8,128)S(1)} %get-tuple-element.12.kc_ref, f32[32,128]{1,0:T(8,128)S(1)} %scatter_obs.1.obs_ref, ...), custom_call_target="tpu_custom_call" | custom-call | tf_op jit(solution)/shard_map/forecast/pallas_call | solution.py:419
  40.5 20.2 %all_to_all.10 = f32[16,20,128]{2,1,0:T(8,128)S(1)} all-to-all(f32[16,20,128]{2,1,0:T(8,128)S(1)} %get-tuple-element.16), channel_id=1, replica_groups=mesh['region'=16,'tile'=32] {'region'}, dimensions={0} | all-to-all | bytes 327680 | tf_op jit(solution)/shard_map/all_to_all | solution.py:433
  60.8 17.3 %all_to_all.11.pay_ref = f32[32,20,128]{2,1,0:T(8,128)S(1)} all-to-all(f32[32,20,128]{2,1,0:T(8,128)S(1)} %broadcast_in_dim.3), channel_id=1, replica_groups=mesh['region'=16,'tile'=32] {'tile'}, dimensions={0} | all-to-all | bytes 655360 | tf_op jit(solution)/shard_map/all_to_all | solution.py:434
  78.0 8.2 %analysis.1 = f32[1024,128]{1,0:T(8,128)} custom-call(f32[32,20,128]{2,1,0:T(8,128)S(1)} %all_to_all.11.pay_ref, f32[64,2048]{1,0:T(8,128)S(1)} %get-tuple-element.17.dev_ref, f32[16,128]{1,0:T(8,128)S(1)} %get-tuple-element.18.mean_ref), custom_call_target="tpu_custom_call" | custom-call | tf_op jit(solution)/shard_map/analysis/pallas_call | solution.py:435
  (8 shorter events, 0.1 us)
Async XLA Ops:
  0.0 0.7 copy-start.7
  0.7 1.0 %copy-start = (f32[64,4,4,128]{3,2,1,0:T(4,128)S(1)}, f32[64,4,4,128]{3,2,1,0:T(4,128)}, u32[]{:S(2)}) copy-start(f32[64,4,4,128]{3,2,1,0:T(4,128)} %param.8) | copy-start | bytes 1572868
  1.7 0.9 %copy-start.2 = (f32[64,4,128]{2,1,0:T(4,128)S(1)}, f32[64,4,128]{2,1,0:T(4,128)}, u32[]{:S(2)}) copy-start(f32[64,4,128]{2,1,0:T(4,128)} %param.9) | copy-start | bytes 393220
  2.6 0.7 copy-start.3
  3.3 29.4 %copy-start.1 = (f32[64,4,4,128]{3,2,1,0:T(4,128)S(1)}, f32[64,4,4,128]{3,2,1,0:T(4,128)}, u32[]{:S(2)}) copy-start(f32[64,4,4,128]{3,2,1,0:T(4,128)} %param.8) | copy-start | bytes 1572868
  4.1 28.5 %collective-permute-start = (f32[984,128]{1,0:T(8,128)S(1)}, f32[984,128]{1,0:T(8,128)S(1)}, u32[]{:S(2)}, u32[]{:S(2)}) collective-permute-start(f32[984,128]{1,0:T(8,128)S(1)} %get-tuple-element.13), channel_id=1, source_target_pairs={{0,32},{32,64},{64,96},{96,128},{128,160},{160,192},{192,224},{224... | collective-permute-start | bytes 1511432 | tf_op jit(solution)/shard_map/ppermute | solution.py:381
  6.8 25.8 %collective-permute-start.1 = (f32[984,128]{1,0:T(8,128)S(1)}, f32[984,128]{1,0:T(8,128)S(1)}, u32[]{:S(2)}, u32[]{:S(2)}) collective-permute-start(f32[984,128]{1,0:T(8,128)S(1)} %get-tuple-element.14), channel_id=1, source_target_pairs={{0,480},{32,0},{64,32},{96,64},{128,96},{160,128},{192,160},{224,1... | collective-permute-start | bytes 1511432 | tf_op jit(solution)/shard_map/ppermute | solution.py:381
  11.1 20.7 %copy-start.5 = (f32[256]{0:T(256)S(1)}, f32[256]{0:T(256)}, u32[]{:S(2)}) copy-start(f32[256]{0:T(256)} %param.13) | copy-start | bytes 3076
  11.1 20.7 %copy-start.6 = (f32[256]{0:T(256)S(1)}, f32[256]{0:T(256)}, u32[]{:S(2)}) copy-start(f32[256]{0:T(256)} %param.14) | copy-start | bytes 3076
  11.1 10.7 %collective-permute-start.3 = (f32[72,128]{1,0:T(8,128)S(1)}, f32[72,128]{1,0:T(8,128)S(1)}, u32[]{:S(2)}, u32[]{:S(2)}) collective-permute-start(f32[72,128]{1,0:T(8,128)S(1)} %get-tuple-element.15.edge_ref), channel_id=1, source_target_pairs={{0,31},{1,0},{2,1},{3,2},{4,3},{5,4},{6,5},{7,6},{8,7},{9,8},{10,9... | collective-permute-start | bytes 110600 | tf_op jit(solution)/shard_map/ppermute | solution.py:381
  19.8 8.0 %collective-permute-start.2 = (f32[72,128]{1,0:T(8,128)S(1)}, f32[72,128]{1,0:T(8,128)S(1)}, u32[]{:S(2)}, u32[]{:S(2)}) collective-permute-start(f32[72,128]{1,0:T(8,128)S(1)} %get-tuple-element.15.edge_ref), channel_id=1, source_target_pairs={{0,1},{1,2},{2,3},{3,4},{4,5},{5,6},{6,7},{7,8},{8,9},{9,10},{10,1... | collective-permute-start | bytes 110600 | tf_op jit(solution)/shard_map/ppermute | solution.py:381
  21.8 9.3 %collective-permute-start.7 = (f32[72,128]{1,0:T(8,128)S(1)}, f32[72,128]{1,0:T(8,128)S(1)}, u32[]{:S(2)}, u32[]{:S(2)}) collective-permute-start(f32[72,128]{1,0:T(8,128)S(1)} %collective-permute-done.3.er_ref), channel_id=1, source_target_pairs={{0,480},{32,0},{64,32},{96,64},{128,96},{160,128},{192,160},{224,1... | collective-permute-start | bytes 110600 | tf_op jit(solution)/shard_map/ppermute | solution.py:381
  23.8 8.8 %collective-permute-start.5 = (f32[72,128]{1,0:T(8,128)S(1)}, f32[72,128]{1,0:T(8,128)S(1)}, u32[]{:S(2)}, u32[]{:S(2)}) collective-permute-start(f32[72,128]{1,0:T(8,128)S(1)} %collective-permute-done.3.er_ref), channel_id=1, source_target_pairs={{0,32},{32,64},{64,96},{96,128},{128,160},{160,192},{192,224},{224... | collective-permute-start | bytes 110600 | tf_op jit(solution)/shard_map/ppermute | solution.py:381
  27.9 4.8 %collective-permute-start.6 = (f32[72,128]{1,0:T(8,128)S(1)}, f32[72,128]{1,0:T(8,128)S(1)}, u32[]{:S(2)}, u32[]{:S(2)}) collective-permute-start(f32[72,128]{1,0:T(8,128)S(1)} %collective-permute-done.2.el_ref), channel_id=1, source_target_pairs={{0,480},{32,0},{64,32},{96,64},{128,96},{160,128},{192,160},{224,1... | collective-permute-start | bytes 110600 | tf_op jit(solution)/shard_map/ppermute | solution.py:381
  31.1 1.6 %collective-permute-start.4 = (f32[72,128]{1,0:T(8,128)S(1)}, f32[72,128]{1,0:T(8,128)S(1)}, u32[]{:S(2)}, u32[]{:S(2)}) collective-permute-start(f32[72,128]{1,0:T(8,128)S(1)} %collective-permute-done.2.el_ref), channel_id=1, source_target_pairs={{0,32},{32,64},{64,96},{96,128},{128,160},{160,192},{192,224},{224... | collective-permute-start | bytes 110600 | tf_op jit(solution)/shard_map/ppermute | solution.py:381
  31.7 0.7 copy-start.4

commit v2 on v1

--- a/solution.py
+++ b/solution.py
@@ -21,7 +21,7 @@
 MSG_KC = MSG_FORCE + 2 * MEM
 MSG_EDGE = MSG_KC + CELLS
 MSG_ROWS = MSG_EDGE + PAD
-PAYLOAD = 20
+PAYLOAD = 5 * COLS
 HIGHEST = lax.Precision.HIGHEST
 F32 = jnp.float32
 
@@ -110,7 +110,7 @@
     h_ref, f_ref, kc_ref, obs_ref, above_ref, below_ref, edge_ref, el_ref, er_ref,
     uel_ref, uer_ref, del_ref, der_ref,
     dev_ref, mean_ref, pay_ref,
-    z_ref, sum_ref, ks_ref, gram_ref,
+    z_ref, ks_ref, kr_ref, face_ref, hold_ref, gram_ref,
 ):
     ri = lax.axis_index("region")
     ti = lax.axis_index("tile")
@@ -150,10 +150,6 @@
         return out
 
     kstrip = strips(lambda ref, base: ref[pl.ds(base + MEM, 8), :])
-    for l in range(LEV):
-        ks_ref[pl.ds(l * 8, 8), :] = kstrip[l]
-    sum_ref[...] = jnp.zeros(sum_ref.shape, F32)
-
     def kc_row(l, e):
         r = e - HALO
         if r < 0:
@@ -165,110 +161,125 @@
         at = l * ROWS + r
         return kc_ref[at : at + 1, :]
 
-    kcs = {(l, e): kc_row(l, e) for l in range(LEV) for e in range(EXT)}
+    for l in range(LEV):
+        ks_ref[pl.ds(l * 8, 8), :] = 0.0625 * kstrip[l]
+        for e in range(EXT):
+            kr_ref[pl.ds((l * EXT + e) * 8, 8), :] = jnp.broadcast_to(
+                0.0625 * kc_row(l, e), (8, COLS)
+            )
 
     def conduct(kc, h):
-        return kc + (0.5 * kc) * jnp.tanh(0.5 * h)
+        return kc * (2.0 + jnp.tanh(0.5 * h))
+
+    joint = is_left & (scol == 1)
 
     def group(g, carry):
         base = g * 8
+
+        def prior_row(l, e):
+            r = e - HALO
+            if r < 0:
+                at = (l * HALO + r + HALO) * MEM
+                return above_ref[pl.ds(at + base, 8), :] * top_ok
+            if r >= ROWS:
+                at = (l * HALO + r - ROWS) * MEM
+                return below_ref[pl.ds(at + base, 8), :] * bot_ok
+            return h_ref[pl.ds(g * (8 * CELLS) + l * ROWS + r, 8, stride=CELLS), :]
+
+        def force_row(e):
+            r = e - HALO
+            if r < 0:
+                return above_ref[pl.ds(MSG_FORCE + (r + 2) * MEM + base, 8), :]
+            if r >= ROWS:
+                return below_ref[pl.ds(MSG_FORCE + (r - ROWS) * MEM + base, 8), :]
+            return f_ref[pl.ds(g * (8 * ROWS) + r, 8, stride=ROWS), :]
+
         hs = strips(lambda ref, first: ref[pl.ds(first + base, 8), :])
         fs = hs[LEV]
-        h = {}
-        force = {}
-        for l in range(LEV):
-            for e in range(EXT):
-                r = e - HALO
-                if r < 0:
-                    at = (l * HALO + r + HALO) * MEM
-                    h[l, e] = above_ref[pl.ds(at + base, 8), :] * top_ok
-                elif r >= ROWS:
-                    at = (l * HALO + r - ROWS) * MEM
-                    h[l, e] = below_ref[pl.ds(at + base, 8), :] * bot_ok
-                else:
-                    h[l, e] = h_ref[pl.ds(g * (8 * CELLS) + l * ROWS + r, 8, stride=CELLS), :]
-        for e in range(1, EXT - 1):
-            r = e - HALO
-            if r < 0:
-                force[e] = above_ref[pl.ds(MSG_FORCE + (r + 2) * MEM + base, 8), :]
-            elif r >= ROWS:
-                force[e] = below_ref[pl.ds(MSG_FORCE + (r - ROWS) * MEM + base, 8), :]
-            else:
-                force[e] = f_ref[pl.ds(g * (8 * ROWS) + r, 8, stride=ROWS), :]
-
         for step in range(STEPS):
-            faces = []
             sk = [conduct(ks_ref[pl.ds(l * 8, 8), :], hs[l]) for l in range(LEV)]
+            faces = [
+                (sk[l] + roll(sk[l], -1)) * (roll(hs[l], -1) - hs[l]) for l in range(LEV)
+            ]
             for l in range(LEV):
-                faces.append((sk[l] + roll(sk[l], -1)) * (roll(hs[l], -1) - hs[l]))
-            if step < STEPS - 1:
-                vert = [
-                    0.5 * (sk[l] + sk[l + 1]) * (hs[l + 1] - hs[l]) for l in range(LEV - 1)
+                edge = jnp.where(joint, roll(faces[l], -65), faces[l])
+                face_ref[pl.ds((step * LEV + l) * 8, 8), :] = edge
+            if step == STEPS - 1:
+                break
+            fresh = []
+            last = None
+            for l in range(LEV):
+                down = (sk[l] + roll(sk[l], -6)) * (roll(hs[l], -6) - hs[l])
+                flux = (faces[l] - roll(faces[l], 1)) + (down - roll(down, 6))
+                if l > 0:
+                    flux = flux - last
+                if l < LEV - 1:
+                    last = 0.5 * (sk[l] + sk[l + 1]) * (hs[l + 1] - hs[l])
+                    flux = flux + last
+                if l == 0:
+                    flux = flux + 0.25 * fs
+                fresh.append((hs[l] + flux) * smask)
+            hs = fresh
+
+        for step in range(STEPS):
+            def row(l, e):
+                if step == 0:
+                    return prior_row(l, e)
+                return hold_ref[step - 1, pl.ds((l * EXT + e) * 8, 8), :]
+
+            h_now = k_now = face_now = None
+            for e in range(step, EXT - step):
+                h_new = [row(l, e) for l in range(LEV)]
+                k_new = [
+                    conduct(kr_ref[pl.ds((l * EXT + e) * 8, 8), :], h_new[l])
+                    for l in range(LEV)
                 ]
-                fresh = []
-                for l in range(LEV):
-                    down = (sk[l] + roll(sk[l], -6)) * (roll(hs[l], -6) - hs[l])
-                    flux = faces[l] - roll(faces[l], 1) + down - roll(down, 6)
-                    if l < LEV - 1:
-                        flux = flux + vert[l]
-                    if l > 0:
-                        flux = flux - vert[l - 1]
-                    flux = 0.125 * flux
-                    if l == 0:
-                        flux = flux + 0.25 * fs
-                    fresh.append((hs[l] + flux) * smask)
-                hs = fresh + [fs]
-            k = {
-                (l, e): conduct(kcs[l, e], h[l, e])
-                for l in range(LEV)
-                for e in range(step, EXT - step)
-            }
-            new = {}
-            rowface = {}
-            for e in range(step, EXT - step):
-                above_vert = None
-                for l in range(LEV):
-                    if e < EXT - step - 1:
-                        rowface[l, e] = (k[l, e] + k[l, e + 1]) * (h[l, e + 1] - h[l, e])
-                    if e == step or e == EXT - step - 1:
-                        continue
-                    here, kh = h[l, e], k[l, e]
-                    face = (kh + roll(kh, -1)) * (roll(here, -1) - here)
-                    face = jnp.where(lane == COLS - 1, roll(faces[l], 61 - e * 6), face)
-                    behind = jnp.where(lane == 0, roll(faces[l], -(e * 6 + 2)), roll(face, 1))
-                    flux = (face - behind) + (rowface[l, e] - rowface[l, e - 1])
-                    if l < LEV - 1:
-                        vert = 0.5 * (kh + k[l + 1, e]) * (h[l + 1, e] - here)
-                        flux = flux + vert
-                    if l > 0:
-                        flux = flux - above_vert
-                    if l < LEV - 1:
-                        above_vert = vert
-                    flux = 0.125 * flux
-                    if l == 0:
-                        flux = flux + 0.25 * force[e]
-                    value = here + flux
-                    if e < HALO:
-                        value = value * top_ok
-                    elif e >= HALO + ROWS:
-                        value = value * bot_ok
-                    new[l, e] = value
-            h = new
-        for l in range(LEV):
-            for r in range(ROWS):
-                lr = l * ROWS + r
-                value = h[l, r + HALO]
-                dev_ref[pl.ds(base, 8), lr * COLS : (lr + 1) * COLS] = value
-                sum_ref[lr * 8 : lr * 8 + 8, :] += value
+                face_new = None
+                if e > step:
+                    face_new = [
+                        (k_now[l] + k_new[l]) * (h_new[l] - h_now[l]) for l in range(LEV)
+                    ]
+                if e > step + 1:
+                    at = e - 1
+                    r = at - HALO
+                    last = None
+                    for l in range(LEV):
+                        here, kh = h_now[l], k_now[l]
+                        edge = roll(
+                            face_ref[pl.ds((step * LEV + l) * 8, 8), :], -(at * 6 + 2)
+                        )
+                        face = (kh + roll(kh, -1)) * (roll(here, -1) - here)
+                        face = jnp.where(lane == COLS - 1, edge, face)
+                        behind = jnp.where(lane == 0, edge, roll(face, 1))
+                        flux = (face - behind) + (face_new[l] - face_now[l])
+                        if l > 0:
+                            flux = flux - last
+                        if l < LEV - 1:
+                            last = 0.5 * (kh + k_now[l + 1]) * (h_now[l + 1] - here)
+                            flux = flux + last
+                        if l == 0:
+                            flux = flux + 0.25 * force_row(at)
+                        value = here + flux
+                        if step == STEPS - 1:
+                            lr = l * ROWS + r
+                            dev_ref[pl.ds(base, 8), lr * COLS : (lr + 1) * COLS] = value
+                            continue
+                        if r < 0:
+                            value = value * top_ok
+                        elif r >= ROWS:
+                            value = value * bot_ok
+                        hold_ref[step, pl.ds((l * EXT + at) * 8, 8), :] = value
+                h_now, k_now, face_now = h_new, k_new, face_new
         return carry
 
     lax.fori_loop(0, GROUPS, group, 0)
 
     for lr in range(CELLS):
-        mean = jnp.sum(sum_ref[lr * 8 : lr * 8 + 8, :], axis=0, keepdims=True) * (1.0 / MEM)
+        cols = slice(lr * COLS, (lr + 1) * COLS)
+        head = dev_ref[:, cols]
+        mean = jnp.sum(head, axis=0, keepdims=True) * (1.0 / MEM)
         mean_ref[lr : lr + 1, :] = mean
-        cols = slice(lr * COLS, (lr + 1) * COLS)
-        dev = dev_ref[:, cols] - mean
+        dev = head - mean
         dev_ref[:, cols] = dev
         scale = obs_ref[lr : lr + 1, :]
         z_ref[0:MEM, cols] = dev * scale
@@ -299,21 +310,20 @@
         lane[0:4] < MEM, last[0:4], roll(last[4:8], MEM)
     )
     for c in range(regions):
-        pay_ref[c, 0:8, :] = first
-        pay_ref[c, 8:16, :] = second
-        pay_ref[c, 16:20, :] = third
+        for i, piece in enumerate((first[0:4], first[4:8], second[0:4], second[4:8], third)):
+            pay_ref[c, :, i * COLS : (i + 1) * COLS] = piece
 
 
 def analysis_kernel(copies, pay_ref, dev_ref, mean_ref, out_ref, m_ref):
     lane = lanes()
     sub = lax.broadcasted_iota(jnp.int32, (8, COLS), 0)
-    first = pay_ref[0, 0:8, :]
-    second = pay_ref[0, 8:16, :]
-    third = pay_ref[0, 16:20, :]
+    total = pay_ref[0]
     for c in range(1, copies):
-        first = first + pay_ref[c, 0:8, :]
-        second = second + pay_ref[c, 8:16, :]
-        third = third + pay_ref[c, 16:20, :]
+        total = total + pay_ref[c]
+    piece = [total[:, i * COLS : (i + 1) * COLS] for i in range(5)]
+    first = jnp.concatenate(piece[0:2], axis=0)
+    second = jnp.concatenate(piece[2:4], axis=0)
+    third = piece[4]
     halves = [
         first,
         roll(first, MEM),
@@ -335,14 +345,23 @@
 
     for kb in range(8):
         block = m_ref[8 * kb : 8 * kb + 8, :]
+        at = 8 * kb
+        full = {
+            (i, j): jnp.broadcast_to(block[i : i + 1, at + j : at + j + 1], (8, COLS))
+            for i in range(8)
+            for j in range(i + 1)
+        }
         for j in range(8):
-            at = 8 * kb + j
-            inv = lax.rsqrt(block[j : j + 1, at : at + 1])
-            prow = block[j : j + 1, :] * inv
-            factor = block[:, at : at + 1] * inv
-            block = jnp.where(
-                sub > j, block - factor * prow, jnp.where(sub == j, prow, block)
-            )
+            inv = lax.rsqrt(full[j, j])
+            low = {i: full[i, j] * inv for i in range(j + 1, 8)}
+            for i in range(j + 1, 8):
+                for m in range(j + 1, i + 1):
+                    full[i, m] = full[i, m] - low[i] * low[m]
+            prow = jnp.broadcast_to(block[j : j + 1, :], (8, COLS)) * inv
+            column = jnp.zeros((8, COLS), F32)
+            for i in range(j + 1, 8):
+                column = jnp.where(sub == i, low[i], column)
+            block = jnp.where(sub == j, prow, block - column * prow)
         m_ref[8 * kb : 8 * kb + 8, :] = block
         if kb < 7:
             later = 8 * (kb + 1)
@@ -418,13 +437,15 @@
     )
     dev, mean, pay = pl.pallas_call(
         functools.partial(forecast_kernel, regions, tiles),
-        out_shape=(out(MEM, CELLS * COLS), out(CELLS, COLS), out(regions, PAYLOAD, COLS)),
+        out_shape=(out(MEM, CELLS * COLS), out(CELLS, COLS), out(regions, 4, PAYLOAD)),
         in_specs=[vmem()] * 13,
         out_specs=(vmem(),) * 3,
         scratch_shapes=[
             pltpu.VMEM((PAD, CELLS * COLS), F32),
-            pltpu.VMEM((CELLS * 8, COLS), F32),
             pltpu.VMEM((LEV * 8, COLS), F32),
+            pltpu.VMEM((LEV * EXT * 8, COLS), F32),
+            pltpu.VMEM((STEPS * LEV * 8, COLS), F32),
+            pltpu.VMEM((STEPS - 1, LEV * EXT * 8, COLS), F32),
             pltpu.VMEM((PAD, COLS), F32),
         ],
         compiler_params=PARAMS,

time: 86.6 us -> 80.7 us (0.932)
  Pallas kernels: 17.1 us -> 13.3 us
  blocking collectives: 37.5 us -> 35.3 us
    pallas_call x1, Pallas kernels: 8.23 us -> 4.87 us  [shards(): pl.pallas_call(functools.partial(analysis_kernel, tiles), out_shape=out(M...]
    all_to_all x1, blocking collectives: 17.3 us -> 15.7 us  [shards(): lax.all_to_all(jnp.broadcast_to(part, (tiles,) + part.shape), 'tile', 0, 0)]
where the time goes in v2:
time: 80.7 us; the launch traced here: 80.3 us
  blocking collectives  35.3 us (44%)
  starting transfers between devices  22.9 us (28%)
  Pallas kernels  13.3 us (16%)
  waiting for transfers between devices  4.06 us (5%)
  local copies, waits for them, and re-layouts  4.01 us (5%)
    ppermute x8, starting transfers between devices, shift(): return lax.ppermute(x, axis, [(i, (i + by) % count) for i in range(count)])  22.9 us
    all_to_all x1, blocking collectives, shards(): part = lax.all_to_all(pay, 'region', 0, 0).sum(axis=0)  19.5 us
    all_to_all x1, blocking collectives, shards(): lax.all_to_all(jnp.broadcast_to(part, (tiles,) + part.shape), 'tile', 0, 0)  15.7 us
    pallas_call x1, Pallas kernels, shards(): pl.pallas_call(functools.partial(forecast_kernel, regions, tiles), out_sh...  7.37 us
    pallas_call x1, Pallas kernels, shards(): pl.pallas_call(functools.partial(analysis_kernel, tiles), out_shape=out(M...  4.87 us
    ppermute x8, waiting for transfers between devices, shift(): return lax.ppermute(x, axis, [(i, (i + by) % count) for i in range(count)])  4.06 us
    unnamed x16, local copies, waits for them, and re-layouts  3.96 us
  transfers between devices with their start and end apart: 8, of which 1 were waited for; matrix products, arithmetic and copies ran while one was open for 0% of the time, Pallas kernels for 0%

profile of v2, /device:TPU:1, one launch (start us, length us, event | category | flops | bytes accessed | tf_op | source)
XLA Modules:
  0.0 80.3 jit_solution(14840759065421879201)
XLA Ops:
  0.0 0.0 copy-start.7
  0.0 0.7 copy-done.7
  0.7 1.0 %copy-done = f32[64,4,4,128]{3,2,1,0:T(4,128)S(1)} copy-done((f32[64,4,4,128]{3,2,1,0:T(4,128)S(1)}, f32[64,4,4,128]{3,2,1,0:T(4,128)}, u32[]{:S(2)}) %copy-start) | copy-done | bytes 524312
  1.7 0.9 %copy-done.2 = f32[64,4,128]{2,1,0:T(4,128)S(1)} copy-done((f32[64,4,128]{2,1,0:T(4,128)S(1)}, f32[64,4,128]{2,1,0:T(4,128)}, u32[]{:S(2)}) %copy-start.2) | copy-done | bytes 131096
  2.6 0.7 copy-done.3
  3.3 0.8 %pack.1 = (f32[984,128]{1,0:T(8,128)S(1)}, f32[984,128]{1,0:T(8,128)S(1)}, f32[72,128]{1,0:T(8,128)S(1)}, f32[16,128]{1,0:T(8,128)S(1)}) custom-call(f32[1024,128]{1,0:T(8,128)S(1)} %bitcast.7, f32[256,128]{1,0:T(8,128)S(1)} %bitcast.9, s32[16,128]{1,0:T(8,128)S(1)} %bitcast.11, f32[12]{0:T(128)S(1)} %copy-done.7), custom_call_target="tpu_custom_call" | custom-call | tf_op jit(solution)/shard_map/pack/pallas_call | solution.py:413
  4.1 2.7 %collective-permute-start = (f32[984,128]{1,0:T(8,128)S(1)}, f32[984,128]{1,0:T(8,128)S(1)}, u32[]{:S(2)}, u32[]{:S(2)}) collective-permute-start(f32[984,128]{1,0:T(8,128)S(1)} %get-tuple-element.13), channel_id=1, source_target_pairs={{0,32},{32,64},{64,96},{96,128},{128,160},{160,192},{192,224},{224... | collective-permute-start | bytes 1511432 | tf_op jit(solution)/shard_map/ppermute | solution.py:400
  6.8 4.2 %collective-permute-start.1 = (f32[984,128]{1,0:T(8,128)S(1)}, f32[984,128]{1,0:T(8,128)S(1)}, u32[]{:S(2)}, u32[]{:S(2)}) collective-permute-start(f32[984,128]{1,0:T(8,128)S(1)} %get-tuple-element.14), channel_id=1, source_target_pairs={{0,480},{32,0},{64,32},{96,64},{128,96},{160,128},{192,160},{224,1... | collective-permute-start | bytes 1511432 | tf_op jit(solution)/shard_map/ppermute | solution.py:400
  11.1 8.8 %collective-permute-start.3 = (f32[72,128]{1,0:T(8,128)S(1)}, f32[72,128]{1,0:T(8,128)S(1)}, u32[]{:S(2)}, u32[]{:S(2)}) collective-permute-start(f32[72,128]{1,0:T(8,128)S(1)} %get-tuple-element.15.edge_ref), channel_id=1, source_target_pairs={{0,31},{1,0},{2,1},{3,2},{4,3},{5,4},{6,5},{7,6},{8,7},{9,8},{10,9... | collective-permute-start | bytes 110600 | tf_op jit(solution)/shard_map/ppermute | solution.py:400
  19.8 1.9 %collective-permute-start.2 = (f32[72,128]{1,0:T(8,128)S(1)}, f32[72,128]{1,0:T(8,128)S(1)}, u32[]{:S(2)}, u32[]{:S(2)}) collective-permute-start(f32[72,128]{1,0:T(8,128)S(1)} %get-tuple-element.15.edge_ref), channel_id=1, source_target_pairs={{0,1},{1,2},{2,3},{3,4},{4,5},{5,6},{6,7},{7,8},{8,9},{9,10},{10,1... | collective-permute-start | bytes 110600 | tf_op jit(solution)/shard_map/ppermute | solution.py:400
  21.8 0.0 collective-permute-done.3.er_ref
  21.8 2.1 %collective-permute-start.7 = (f32[72,128]{1,0:T(8,128)S(1)}, f32[72,128]{1,0:T(8,128)S(1)}, u32[]{:S(2)}, u32[]{:S(2)}) collective-permute-start(f32[72,128]{1,0:T(8,128)S(1)} %collective-permute-done.3.er_ref), channel_id=1, source_target_pairs={{0,480},{32,0},{64,32},{96,64},{128,96},{160,128},{192,160},{224,1... | collective-permute-start | bytes 110600 | tf_op jit(solution)/shard_map/ppermute | solution.py:400
  23.8 0.0 collective-permute-start.5
  23.8 4.0 %collective-permute-done.2.el_ref = f32[72,128]{1,0:T(8,128)S(1)} collective-permute-done((f32[72,128]{1,0:T(8,128)S(1)}, f32[72,128]{1,0:T(8,128)S(1)}, u32[]{:S(2)}, u32[]{:S(2)}) %collective-permute-start.2) | collective-permute-done | bytes 36896 | tf_op jit(solution)/shard_map/ppermute | solution.py:400
  27.9 3.2 %collective-permute-start.6 = (f32[72,128]{1,0:T(8,128)S(1)}, f32[72,128]{1,0:T(8,128)S(1)}, u32[]{:S(2)}, u32[]{:S(2)}) collective-permute-start(f32[72,128]{1,0:T(8,128)S(1)} %collective-permute-done.2.el_ref), channel_id=1, source_target_pairs={{0,480},{32,0},{64,32},{96,64},{128,96},{160,128},{192,160},{224,1... | collective-permute-start | bytes 110600 | tf_op jit(solution)/shard_map/ppermute | solution.py:400
  31.1 0.0 collective-permute-done.7.der_ref
  31.1 0.0 collective-permute-start.4
  31.7 0.0 copy-start.4
  31.7 0.0 copy-done.5
  31.7 0.0 copy-done.6
  31.7 0.7 copy-done.4
  32.4 0.2 scatter_obs.1.obs_ref
  32.6 0.0 collective-permute-done.5.uer_ref
  32.6 0.0 collective-permute-done.6.del_ref
  32.7 0.0 collective-permute-done.4.uel_ref
  32.7 0.0 collective-permute-done.above_ref
  32.7 0.0 collective-permute-done.1.below_ref
  32.7 0.0 copy-done.1
  32.7 7.4 %forecast.1 = (f32[64,2048]{1,0:T(8,128)S(1)}, f32[16,128]{1,0:T(8,128)S(1)}, f32[16,4,640]{2,1,0:T(4,128)S(1)}) custom-call(f32[1024,128]{1,0:T(8,128)S(1)} %bitcast.8, f32[256,128]{1,0:T(8,128)S(1)} %bitcast.10, f32[16,128]{1,0:T(8,128)S(1)} %get-tuple-element.12.kc_ref, f32[32,128]{1,0:T(8,128)S(1)} %scatter_obs.1.obs_ref, ...), custom_call_target="tpu_custom_call" | custom-call | tf_op jit(solution)/shard_map/forecast/pallas_call | solution.py:438
  40.1 19.5 %all_to_all.10 = f32[16,4,640]{2,1,0:T(4,128)S(1)} all-to-all(f32[16,4,640]{2,1,0:T(4,128)S(1)} %get-tuple-element.16), channel_id=1, replica_groups=mesh['region'=16,'tile'=32] {'region'}, dimensions={0} | all-to-all | bytes 327680 | tf_op jit(solution)/shard_map/all_to_all | solution.py:454
  59.7 15.7 %all_to_all.11.pay_ref = f32[32,4,640]{2,1,0:T(4,128)S(1)} all-to-all(f32[32,4,640]{2,1,0:T(4,128)S(1)} %broadcast_in_dim.3), channel_id=1, replica_groups=mesh['region'=16,'tile'=32] {'tile'}, dimensions={0} | all-to-all | bytes 655360 | tf_op jit(solution)/shard_map/all_to_all | solution.py:455
  75.4 4.9 %analysis.1 = f32[1024,128]{1,0:T(8,128)} custom-call(f32[32,4,640]{2,1,0:T(4,128)S(1)} %all_to_all.11.pay_ref, f32[64,2048]{1,0:T(8,128)S(1)} %get-tuple-element.17.dev_ref, f32[16,128]{1,0:T(8,128)S(1)} %get-tuple-element.18.mean_ref), custom_call_target="tpu_custom_call" | custom-call | tf_op jit(solution)/shard_map/analysis/pallas_call | solution.py:456
  (8 shorter events, 0.1 us)
Async XLA Ops:
  0.0 0.7 copy-start.7
  0.7 1.0 %copy-start = (f32[64,4,4,128]{3,2,1,0:T(4,128)S(1)}, f32[64,4,4,128]{3,2,1,0:T(4,128)}, u32[]{:S(2)}) copy-start(f32[64,4,4,128]{3,2,1,0:T(4,128)} %param.8) | copy-start | bytes 1572868
  1.7 0.9 %copy-start.2 = (f32[64,4,128]{2,1,0:T(4,128)S(1)}, f32[64,4,128]{2,1,0:T(4,128)}, u32[]{:S(2)}) copy-start(f32[64,4,128]{2,1,0:T(4,128)} %param.9) | copy-start | bytes 393220
  2.6 0.7 copy-start.3
  3.3 29.4 %copy-start.1 = (f32[64,4,4,128]{3,2,1,0:T(4,128)S(1)}, f32[64,4,4,128]{3,2,1,0:T(4,128)}, u32[]{:S(2)}) copy-start(f32[64,4,4,128]{3,2,1,0:T(4,128)} %param.8) | copy-start | bytes 1572868
  4.1 28.5 %collective-permute-start = (f32[984,128]{1,0:T(8,128)S(1)}, f32[984,128]{1,0:T(8,128)S(1)}, u32[]{:S(2)}, u32[]{:S(2)}) collective-permute-start(f32[984,128]{1,0:T(8,128)S(1)} %get-tuple-element.13), channel_id=1, source_target_pairs={{0,32},{32,64},{64,96},{96,128},{128,160},{160,192},{192,224},{224... | collective-permute-start | bytes 1511432 | tf_op jit(solution)/shard_map/ppermute | solution.py:400
  6.8 25.8 %collective-permute-start.1 = (f32[984,128]{1,0:T(8,128)S(1)}, f32[984,128]{1,0:T(8,128)S(1)}, u32[]{:S(2)}, u32[]{:S(2)}) collective-permute-start(f32[984,128]{1,0:T(8,128)S(1)} %get-tuple-element.14), channel_id=1, source_target_pairs={{0,480},{32,0},{64,32},{96,64},{128,96},{160,128},{192,160},{224,1... | collective-permute-start | bytes 1511432 | tf_op jit(solution)/shard_map/ppermute | solution.py:400
  11.1 20.7 %copy-start.5 = (f32[256]{0:T(256)S(1)}, f32[256]{0:T(256)}, u32[]{:S(2)}) copy-start(f32[256]{0:T(256)} %param.13) | copy-start | bytes 3076
  11.1 20.7 %copy-start.6 = (f32[256]{0:T(256)S(1)}, f32[256]{0:T(256)}, u32[]{:S(2)}) copy-start(f32[256]{0:T(256)} %param.14) | copy-start | bytes 3076
  11.1 10.7 %collective-permute-start.3 = (f32[72,128]{1,0:T(8,128)S(1)}, f32[72,128]{1,0:T(8,128)S(1)}, u32[]{:S(2)}, u32[]{:S(2)}) collective-permute-start(f32[72,128]{1,0:T(8,128)S(1)} %get-tuple-element.15.edge_ref), channel_id=1, source_target_pairs={{0,31},{1,0},{2,1},{3,2},{4,3},{5,4},{6,5},{7,6},{8,7},{9,8},{10,9... | collective-permute-start | bytes 110600 | tf_op jit(solution)/shard_map/ppermute | solution.py:400
  19.8 8.0 %collective-permute-start.2 = (f32[72,128]{1,0:T(8,128)S(1)}, f32[72,128]{1,0:T(8,128)S(1)}, u32[]{:S(2)}, u32[]{:S(2)}) collective-permute-start(f32[72,128]{1,0:T(8,128)S(1)} %get-tuple-element.15.edge_ref), channel_id=1, source_target_pairs={{0,1},{1,2},{2,3},{3,4},{4,5},{5,6},{6,7},{7,8},{8,9},{9,10},{10,1... | collective-permute-start | bytes 110600 | tf_op jit(solution)/shard_map/ppermute | solution.py:400
  21.8 9.3 %collective-permute-start.7 = (f32[72,128]{1,0:T(8,128)S(1)}, f32[72,128]{1,0:T(8,128)S(1)}, u32[]{:S(2)}, u32[]{:S(2)}) collective-permute-start(f32[72,128]{1,0:T(8,128)S(1)} %collective-permute-done.3.er_ref), channel_id=1, source_target_pairs={{0,480},{32,0},{64,32},{96,64},{128,96},{160,128},{192,160},{224,1... | collective-permute-start | bytes 110600 | tf_op jit(solution)/shard_map/ppermute | solution.py:400
  23.8 8.8 %collective-permute-start.5 = (f32[72,128]{1,0:T(8,128)S(1)}, f32[72,128]{1,0:T(8,128)S(1)}, u32[]{:S(2)}, u32[]{:S(2)}) collective-permute-start(f32[72,128]{1,0:T(8,128)S(1)} %collective-permute-done.3.er_ref), channel_id=1, source_target_pairs={{0,32},{32,64},{64,96},{96,128},{128,160},{160,192},{192,224},{224... | collective-permute-start | bytes 110600 | tf_op jit(solution)/shard_map/ppermute | solution.py:400
  27.9 4.8 %collective-permute-start.6 = (f32[72,128]{1,0:T(8,128)S(1)}, f32[72,128]{1,0:T(8,128)S(1)}, u32[]{:S(2)}, u32[]{:S(2)}) collective-permute-start(f32[72,128]{1,0:T(8,128)S(1)} %collective-permute-done.2.el_ref), channel_id=1, source_target_pairs={{0,480},{32,0},{64,32},{96,64},{128,96},{160,128},{192,160},{224,1... | collective-permute-start | bytes 110600 | tf_op jit(solution)/shard_map/ppermute | solution.py:400
  31.1 1.6 %collective-permute-start.4 = (f32[72,128]{1,0:T(8,128)S(1)}, f32[72,128]{1,0:T(8,128)S(1)}, u32[]{:S(2)}, u32[]{:S(2)}) collective-permute-start(f32[72,128]{1,0:T(8,128)S(1)} %collective-permute-done.2.el_ref), channel_id=1, source_target_pairs={{0,32},{32,64},{64,96},{96,128},{128,160},{160,192},{192,224},{224... | collective-permute-start | bytes 110600 | tf_op jit(solution)/shard_map/ppermute | solution.py:400
  31.7 0.7 copy-start.4

commit v3 on v2

--- a/solution.py
+++ b/solution.py
@@ -48,12 +48,32 @@
     return out
 
 
-def pack_kernel(h_ref, f_ref, cls_ref, k_ref, up_ref, dn_ref, edge_ref, kc_ref):
+def scatter_obs(idx_ref, val_ref, var_ref, count):
+    slots = idx_ref.shape[1]
+    idx = idx_ref[...]
+    slot = lax.broadcasted_iota(jnp.int32, (1, slots), 1)
+    weight = jnp.where(slot < count, 1.0 / var_ref[...], 0.0)
+    place = lax.broadcasted_iota(jnp.int32, (CELLS, slots), 0) == idx // COLS
+    lhs = jnp.concatenate(
+        [jnp.where(place, weight, 0.0), jnp.where(place, weight * val_ref[...], 0.0)], axis=0
+    )
+    rhs = jnp.where(
+        lax.broadcasted_iota(jnp.int32, (COLS, slots), 0) == idx % COLS, 1.0, 0.0
+    )
+    return lax.dot_general(
+        lhs, rhs, (((1,), (1,)), ((), ())), precision=HIGHEST, preferred_element_type=F32
+    )
+
+
+def pack_kernel(
+    h_ref, f_ref, cls_ref, idx_ref, val_ref, var_ref, k_ref, cnt_ref,
+    up_ref, dn_ref, own_ref, edge_ref,
+):
     cls = cls_ref[...]
     kc = jnp.zeros(cls.shape, F32)
     for index in range(12):
         kc = jnp.where(cls == index, k_ref[index], kc)
-    kc_ref[...] = kc
+    own_ref[pl.ds(PAD, CELLS), :] = kc
     up_ref[pl.ds(MSG_KC, CELLS), :] = kc
     dn_ref[pl.ds(MSG_KC, CELLS), :] = kc
     kedge = edge_pack(
@@ -62,9 +82,13 @@
         else jnp.broadcast_to(kc[l * ROWS + r : l * ROWS + r + 1, :], (8, COLS))
     )
     edge_ref[pl.ds(MEM, 8), :] = kedge
+    own_ref[pl.ds(MEM, 8), :] = kedge
     up_ref[pl.ds(MSG_EDGE + MEM, 8), :] = kedge
     dn_ref[pl.ds(MSG_EDGE + MEM, 8), :] = kedge
 
+    own_ref[pl.ds(PAD + CELLS, 2 * CELLS), :] = scatter_obs(
+        idx_ref, val_ref, var_ref, cnt_ref[0]
+    )
     for g in range(GROUPS):
         h = {}
         for l in range(LEV):
@@ -84,30 +108,14 @@
                 dn_ref[pl.ds(MSG_FORCE + (r - 2) * MEM + g * 8, 8), :] = block
         edge = edge_pack(lambda l, r: h[l, r])
         edge_ref[pl.ds(g * 8, 8), :] = edge
+        own_ref[pl.ds(g * 8, 8), :] = edge
         up_ref[pl.ds(MSG_EDGE + g * 8, 8), :] = edge
         dn_ref[pl.ds(MSG_EDGE + g * 8, 8), :] = edge
 
 
-def obs_kernel(idx_ref, val_ref, var_ref, cnt_ref, out_ref):
-    slots = idx_ref.shape[1]
-    idx = idx_ref[...]
-    slot = lax.broadcasted_iota(jnp.int32, (1, slots), 1)
-    weight = jnp.where(slot < cnt_ref[0], 1.0 / var_ref[...], 0.0)
-    high = idx // COLS
-    low = idx % COLS
-    place = lax.broadcasted_iota(jnp.int32, (CELLS, slots), 0) == high
-    lhs = jnp.concatenate(
-        [jnp.where(place, weight, 0.0), jnp.where(place, weight * val_ref[...], 0.0)], axis=0
-    )
-    rhs = jnp.where(lax.broadcasted_iota(jnp.int32, (COLS, slots), 0) == low, 1.0, 0.0)
-    out_ref[...] = lax.dot_general(
-        lhs, rhs, (((1,), (1,)), ((), ())), precision=HIGHEST, preferred_element_type=F32
-    )
-
-
 def forecast_kernel(
     regions, tiles,
-    h_ref, f_ref, kc_ref, obs_ref, above_ref, below_ref, edge_ref, el_ref, er_ref,
+    h_ref, f_ref, own_ref, above_ref, below_ref, el_ref, er_ref,
     uel_ref, uer_ref, del_ref, der_ref,
     dev_ref, mean_ref, pay_ref,
     z_ref, ks_ref, kr_ref, face_ref, hold_ref, gram_ref,
@@ -131,7 +139,7 @@
     low_k = lane % 6 < 3
 
     def strips(base):
-        own, left, right = base(edge_ref, 0), base(el_ref, 0), base(er_ref, 0)
+        own, left, right = base(own_ref, 0), base(el_ref, 0), base(er_ref, 0)
         uown, ul, ur = base(above_ref, MSG_EDGE), base(uel_ref, 0), base(uer_ref, 0)
         down, dl, dr = base(below_ref, MSG_EDGE), base(del_ref, 0), base(der_ref, 0)
         parts = (
@@ -158,8 +166,8 @@
         if r >= ROWS:
             at = MSG_KC + l * ROWS + r - ROWS
             return below_ref[at : at + 1, :] * bot_ok
-        at = l * ROWS + r
-        return kc_ref[at : at + 1, :]
+        at = PAD + l * ROWS + r
+        return own_ref[at : at + 1, :]
 
     for l in range(LEV):
         ks_ref[pl.ds(l * 8, 8), :] = 0.0625 * kstrip[l]
@@ -281,9 +289,9 @@
         mean_ref[lr : lr + 1, :] = mean
         dev = head - mean
         dev_ref[:, cols] = dev
-        scale = obs_ref[lr : lr + 1, :]
+        scale = own_ref[PAD + CELLS + lr : PAD + CELLS + lr + 1, :]
         z_ref[0:MEM, cols] = dev * scale
-        rest = obs_ref[CELLS + lr : CELLS + lr + 1, :] - scale * mean
+        rest = own_ref[PAD + 2 * CELLS + lr : PAD + 2 * CELLS + lr + 1, :] - scale * mean
         z_ref[MEM : MEM + 8, cols] = jnp.broadcast_to(rest, (8, COLS))
     gram_ref[:, 0:MEM] = lax.dot_general(
         z_ref[...], dev_ref[...], (((1,), (1,)), ((), ())),
@@ -395,9 +403,10 @@
 PARAMS = pltpu.CompilerParams(vmem_limit_bytes=32 * 1024 * 1024)
 
 
-def shift(x, axis, by):
+def shift(x, axis, by, wrap=True):
     count = lax.axis_size(axis)
-    return lax.ppermute(x, axis, [(i, (i + by) % count) for i in range(count)])
+    pairs = [(i, (i + by) % count) for i in range(count) if wrap or 0 <= i + by < count]
+    return lax.ppermute(x, axis, pairs)
 
 
 def shards(prior, source, soil_class, soil_k, obs_index, obs_value, obs_var, obs_count):
@@ -410,35 +419,30 @@
     def out(*shape):
         return jax.ShapeDtypeStruct(shape, F32)
 
-    up, dn, edge, kc = pl.pallas_call(
+    up, dn, own, edge = pl.pallas_call(
         pack_kernel,
-        out_shape=(out(MSG_ROWS, COLS), out(MSG_ROWS, COLS), out(PAD, COLS), out(CELLS, COLS)),
-        in_specs=[vmem(), vmem(), vmem(), smem()],
+        out_shape=(
+            out(MSG_ROWS, COLS), out(MSG_ROWS, COLS), out(PAD + 3 * CELLS, COLS), out(PAD, COLS)
+        ),
+        in_specs=[vmem()] * 6 + [smem()] * 2,
         out_specs=(vmem(),) * 4,
         compiler_params=PARAMS,
         name="pack",
-    )(prior, source, soil_class, soil_k)
+    )(
+        prior, source, soil_class,
+        obs_index.reshape(1, slots), obs_value.reshape(1, slots), obs_var.reshape(1, slots),
+        soil_k, obs_count,
+    )
     above = shift(dn, "region", 1)
     below = shift(up, "region", -1)
-    el = shift(edge, "tile", 1)
-    er = shift(edge, "tile", -1)
+    el = shift(edge, "tile", 1, False)
+    er = shift(edge, "tile", -1, False)
     uel, uer = shift(el, "region", 1), shift(er, "region", 1)
     bel, ber = shift(el, "region", -1), shift(er, "region", -1)
-    obs = pl.pallas_call(
-        obs_kernel,
-        out_shape=out(2 * CELLS, COLS),
-        in_specs=[vmem(), vmem(), vmem(), smem()],
-        out_specs=vmem(),
-        compiler_params=PARAMS,
-        name="scatter_obs",
-    )(
-        obs_index.reshape(1, slots), obs_value.reshape(1, slots), obs_var.reshape(1, slots),
-        obs_count,
-    )
     dev, mean, pay = pl.pallas_call(
         functools.partial(forecast_kernel, regions, tiles),
         out_shape=(out(MEM, CELLS * COLS), out(CELLS, COLS), out(regions, 4, PAYLOAD)),
-        in_specs=[vmem()] * 13,
+        in_specs=[vmem()] * 11,
         out_specs=(vmem(),) * 3,
         scratch_shapes=[
             pltpu.VMEM((PAD, CELLS * COLS), F32),
@@ -450,7 +454,7 @@
         ],
         compiler_params=PARAMS,
         name="forecast",
-    )(prior, source, kc, obs, above, below, edge, el, er, uel, uer, bel, ber)
+    )(prior, source, own, above, below, el, er, uel, uer, bel, ber)
     part = lax.all_to_all(pay, "region", 0, 0).sum(axis=0)
     pay = lax.all_to_all(jnp.broadcast_to(part, (tiles,) + part.shape), "tile", 0, 0)
     result = pl.pallas_call(

time: 80.7 us -> 78.5 us (0.973)
  blocking collectives: 35.3 us -> 42 us
  starting transfers between devices: 22.9 us -> 17.4 us
  waiting for transfers between devices: 4.06 us -> 1.95 us
  local copies, waits for them, and re-layouts: 4.01 us -> 2.67 us
    all_to_all x1, blocking collectives: 15.7 us -> 25.9 us  [shards(): lax.all_to_all(jnp.broadcast_to(part, (tiles,) + part.shape), 'tile', 0, 0)]
    ppermute x8, starting transfers between devices: 22.9 us -> 17.4 us  [shift(): return lax.ppermute(x, axis, pairs)]
    all_to_all x1, blocking collectives: 19.5 us -> 16.2 us  [shards(): part = lax.all_to_all(pay, 'region', 0, 0).sum(axis=0)]
    ppermute x8, waiting for transfers between devices: 4.06 us -> 1.95 us  [shift(): return lax.ppermute(x, axis, pairs)]
    unnamed x16 -> x14, local copies, waits for them, and re-layouts: 3.96 us -> 2.62 us
where the time goes in v3:
time: 78.5 us; the launch traced here: 78 us
  blocking collectives  42 us (54%)
  starting transfers between devices  17.4 us (22%)
  Pallas kernels  13.1 us (17%)
  local copies, waits for them, and re-layouts  2.67 us (3%)
  waiting for transfers between devices  1.95 us (2%)
    all_to_all x1, blocking collectives, shards(): lax.all_to_all(jnp.broadcast_to(part, (tiles,) + part.shape), 'tile', 0, 0)  25.9 us
    ppermute x8, starting transfers between devices, shift(): return lax.ppermute(x, axis, pairs)  17.4 us
    all_to_all x1, blocking collectives, shards(): part = lax.all_to_all(pay, 'region', 0, 0).sum(axis=0)  16.2 us
    pallas_call x1, Pallas kernels, shards(): pl.pallas_call(functools.partial(forecast_kernel, regions, tiles), out_sh...  7.35 us
    pallas_call x1, Pallas kernels, shards(): pl.pallas_call(functools.partial(analysis_kernel, tiles), out_shape=out(M...  4.87 us
    unnamed x14, local copies, waits for them, and re-layouts  2.62 us
    ppermute x8, waiting for transfers between devices, shift(): return lax.ppermute(x, axis, pairs)  1.95 us
  transfers between devices with their start and end apart: 8, of which 1 were waited for; matrix products, arithmetic and copies ran while one was open for 0% of the time, Pallas kernels for 0%

profile of v3, /device:TPU:1, one launch (start us, length us, event | category | flops | bytes accessed | tf_op | source)
XLA Modules:
  0.0 78.0 jit_solution(9153410801818654540)
XLA Ops:
  0.7 0.0 copy-start.4
  0.7 0.0 copy-start.5
  0.7 0.0 copy-start.3
  0.7 0.0 copy-start.6
  0.7 0.0 copy-done.2
  0.7 0.6 copy-done.4
  1.3 0.0 copy-done.5
  1.4 0.0 copy-done.3
  1.4 0.0 copy-done.6
  1.4 1.0 %copy-done = f32[64,4,4,128]{3,2,1,0:T(4,128)S(1)} copy-done((f32[64,4,4,128]{3,2,1,0:T(4,128)S(1)}, f32[64,4,4,128]{3,2,1,0:T(4,128)}, u32[]{:S(2)}) %copy-start) | copy-done | bytes 524312
  2.4 0.9 %copy-done.1 = f32[64,4,128]{2,1,0:T(4,128)S(1)} copy-done((f32[64,4,128]{2,1,0:T(4,128)S(1)}, f32[64,4,128]{2,1,0:T(4,128)}, u32[]{:S(2)}) %copy-start.1) | copy-done | bytes 131096
  3.3 0.9 %pack.1 = (f32[984,128]{1,0:T(8,128)S(1)}, f32[984,128]{1,0:T(8,128)S(1)}, f32[120,128]{1,0:T(8,128)S(1)}, f32[72,128]{1,0:T(8,128)S(1)}) custom-call(f32[1024,128]{1,0:T(8,128)S(1)} %bitcast.7, f32[256,128]{1,0:T(8,128)S(1)} %bitcast.9, s32[16,128]{1,0:T(8,128)S(1)} %bitcast.11, s32[1,256]{1,0:T(1,128)S(1)} %bitcast.12, f32[1,256]{1,0:T(1,128)S(1)} %bitcast.13, ...), custom_call_target="tpu_custom_call" | custom-call | tf_op jit(solution)/shard_map/pack/pallas_call | solution.py:422
  4.2 2.7 %collective-permute-start = (f32[984,128]{1,0:T(8,128)S(1)}, f32[984,128]{1,0:T(8,128)S(1)}, u32[]{:S(2)}, u32[]{:S(2)}) collective-permute-start(f32[984,128]{1,0:T(8,128)S(1)} %get-tuple-element.13), channel_id=1, source_target_pairs={{0,32},{32,64},{64,96},{96,128},{128,160},{160,192},{192,224},{224... | collective-permute-start | bytes 1511432 | tf_op jit(solution)/shard_map/ppermute | solution.py:409
  6.9 4.2 %collective-permute-start.1 = (f32[984,128]{1,0:T(8,128)S(1)}, f32[984,128]{1,0:T(8,128)S(1)}, u32[]{:S(2)}, u32[]{:S(2)}) collective-permute-start(f32[984,128]{1,0:T(8,128)S(1)} %get-tuple-element.14), channel_id=1, source_target_pairs={{0,480},{32,0},{64,32},{96,64},{128,96},{160,128},{192,160},{224,1... | collective-permute-start | bytes 1511432 | tf_op jit(solution)/shard_map/ppermute | solution.py:409
  11.1 1.3 %collective-permute-start.3 = (f32[72,128]{1,0:T(8,128)S(1)}, f32[72,128]{1,0:T(8,128)S(1)}, u32[]{:S(2)}, u32[]{:S(2)}) collective-permute-start(f32[72,128]{1,0:T(8,128)S(1)} %get-tuple-element.15), channel_id=1, source_target_pairs={{1,0},{2,1},{3,2},{4,3},{5,4},{6,5},{7,6},{8,7},{9,8},{10,9},{11,1... | collective-permute-start | bytes 110600 | tf_op jit(solution)/shard_map/ppermute | solution.py:409
  12.4 4.0 %collective-permute-start.2 = (f32[72,128]{1,0:T(8,128)S(1)}, f32[72,128]{1,0:T(8,128)S(1)}, u32[]{:S(2)}, u32[]{:S(2)}) collective-permute-start(f32[72,128]{1,0:T(8,128)S(1)} %get-tuple-element.15), channel_id=1, source_target_pairs={{0,1},{1,2},{2,3},{3,4},{4,5},{5,6},{6,7},{7,8},{8,9},{9,10},{10,1... | collective-permute-start | bytes 110600 | tf_op jit(solution)/shard_map/ppermute | solution.py:409
  16.4 0.0 collective-permute-done.3.er_ref
  16.4 3.5 %collective-permute-start.7 = (f32[72,128]{1,0:T(8,128)S(1)}, f32[72,128]{1,0:T(8,128)S(1)}, u32[]{:S(2)}, u32[]{:S(2)}) collective-permute-start(f32[72,128]{1,0:T(8,128)S(1)} %collective-permute-done.3.er_ref), channel_id=1, source_target_pairs={{0,480},{32,0},{64,32},{96,64},{128,96},{160,128},{192,160},{224,1... | collective-permute-start | bytes 110600 | tf_op jit(solution)/shard_map/ppermute | solution.py:409
  19.9 0.0 collective-permute-start.5
  19.9 0.0 collective-permute-done.2.el_ref
  19.9 1.6 %collective-permute-start.6 = (f32[72,128]{1,0:T(8,128)S(1)}, f32[72,128]{1,0:T(8,128)S(1)}, u32[]{:S(2)}, u32[]{:S(2)}) collective-permute-start(f32[72,128]{1,0:T(8,128)S(1)} %collective-permute-done.2.el_ref), channel_id=1, source_target_pairs={{0,480},{32,0},{64,32},{96,64},{128,96},{160,128},{192,160},{224,1... | collective-permute-start | bytes 110600 | tf_op jit(solution)/shard_map/ppermute | solution.py:409
  21.5 0.0 collective-permute-done.7.der_ref
  21.5 0.2 collective-permute-start.4
  21.7 0.0 collective-permute-done.5.uer_ref
  21.7 1.9 %collective-permute-done.6.del_ref = f32[72,128]{1,0:T(8,128)S(1)} collective-permute-done((f32[72,128]{1,0:T(8,128)S(1)}, f32[72,128]{1,0:T(8,128)S(1)}, u32[]{:S(2)}, u32[]{:S(2)}) %collective-permute-start.6) | collective-permute-done | bytes 36896 | tf_op jit(solution)/shard_map/ppermute | solution.py:409
  23.6 0.0 collective-permute-done.4.uel_ref
  23.6 0.0 collective-permute-done.above_ref
  23.6 0.0 collective-permute-done.1.below_ref
  23.6 7.4 %forecast.1 = (f32[64,2048]{1,0:T(8,128)S(1)}, f32[16,128]{1,0:T(8,128)S(1)}, f32[16,4,640]{2,1,0:T(4,128)S(1)}) custom-call(f32[1024,128]{1,0:T(8,128)S(1)} %bitcast.8, f32[256,128]{1,0:T(8,128)S(1)} %bitcast.10, f32[120,128]{1,0:T(8,128)S(1)} %get-tuple-element.12.own_ref, f32[984,128]{1,0:T(8,128)S(1)} %collective-permute-done.above_ref, ...), custom_call_target="tpu_custom_call" | custom-call | tf_op jit(solution)/shard_map/forecast/pallas_call | solution.py:442
  31.0 16.2 %all_to_all.10 = f32[16,4,640]{2,1,0:T(4,128)S(1)} all-to-all(f32[16,4,640]{2,1,0:T(4,128)S(1)} %get-tuple-element.16), channel_id=1, replica_groups=mesh['region'=16,'tile'=32] {'region'}, dimensions={0} | all-to-all | bytes 327680 | tf_op jit(solution)/shard_map/all_to_all | solution.py:458
  47.3 25.9 %all_to_all.11.pay_ref = f32[32,4,640]{2,1,0:T(4,128)S(1)} all-to-all(f32[32,4,640]{2,1,0:T(4,128)S(1)} %broadcast_in_dim.3), channel_id=1, replica_groups=mesh['region'=16,'tile'=32] {'tile'}, dimensions={0} | all-to-all | bytes 655360 | tf_op jit(solution)/shard_map/all_to_all | solution.py:459
  73.1 4.9 %analysis.1 = f32[1024,128]{1,0:T(8,128)} custom-call(f32[32,4,640]{2,1,0:T(4,128)S(1)} %all_to_all.11.pay_ref, f32[64,2048]{1,0:T(8,128)S(1)} %get-tuple-element.17.dev_ref, f32[16,128]{1,0:T(8,128)S(1)} %get-tuple-element.18.mean_ref), custom_call_target="tpu_custom_call" | custom-call | tf_op jit(solution)/shard_map/analysis/pallas_call | solution.py:460
  (5 shorter events, 0.1 us)
Async XLA Ops:
  0.0 0.7 copy-start.2
  0.7 0.7 copy-start.4
  0.7 0.7 copy-start.5
  0.7 0.7 copy-start.3
  0.7 0.7 copy-start.6
  1.4 1.0 %copy-start = (f32[64,4,4,128]{3,2,1,0:T(4,128)S(1)}, f32[64,4,4,128]{3,2,1,0:T(4,128)}, u32[]{:S(2)}) copy-start(f32[64,4,4,128]{3,2,1,0:T(4,128)} %param.8) | copy-start | bytes 1572868
  2.4 0.9 %copy-start.1 = (f32[64,4,128]{2,1,0:T(4,128)S(1)}, f32[64,4,128]{2,1,0:T(4,128)}, u32[]{:S(2)}) copy-start(f32[64,4,128]{2,1,0:T(4,128)} %param.9) | copy-start | bytes 393220
  4.2 19.4 %collective-permute-start = (f32[984,128]{1,0:T(8,128)S(1)}, f32[984,128]{1,0:T(8,128)S(1)}, u32[]{:S(2)}, u32[]{:S(2)}) collective-permute-start(f32[984,128]{1,0:T(8,128)S(1)} %get-tuple-element.13), channel_id=1, source_target_pairs={{0,32},{32,64},{64,96},{96,128},{128,160},{160,192},{192,224},{224... | collective-permute-start | bytes 1511432 | tf_op jit(solution)/shard_map/ppermute | solution.py:409
  6.9 16.7 %collective-permute-start.1 = (f32[984,128]{1,0:T(8,128)S(1)}, f32[984,128]{1,0:T(8,128)S(1)}, u32[]{:S(2)}, u32[]{:S(2)}) collective-permute-start(f32[984,128]{1,0:T(8,128)S(1)} %get-tuple-element.14), channel_id=1, source_target_pairs={{0,480},{32,0},{64,32},{96,64},{128,96},{160,128},{192,160},{224,1... | collective-permute-start | bytes 1511432 | tf_op jit(solution)/shard_map/ppermute | solution.py:409
  11.1 5.3 %collective-permute-start.3 = (f32[72,128]{1,0:T(8,128)S(1)}, f32[72,128]{1,0:T(8,128)S(1)}, u32[]{:S(2)}, u32[]{:S(2)}) collective-permute-start(f32[72,128]{1,0:T(8,128)S(1)} %get-tuple-element.15), channel_id=1, source_target_pairs={{1,0},{2,1},{3,2},{4,3},{5,4},{6,5},{7,6},{8,7},{9,8},{10,9},{11,1... | collective-permute-start | bytes 110600 | tf_op jit(solution)/shard_map/ppermute | solution.py:409
  12.4 7.5 %collective-permute-start.2 = (f32[72,128]{1,0:T(8,128)S(1)}, f32[72,128]{1,0:T(8,128)S(1)}, u32[]{:S(2)}, u32[]{:S(2)}) collective-permute-start(f32[72,128]{1,0:T(8,128)S(1)} %get-tuple-element.15), channel_id=1, source_target_pairs={{0,1},{1,2},{2,3},{3,4},{4,5},{5,6},{6,7},{7,8},{8,9},{9,10},{10,1... | collective-permute-start | bytes 110600 | tf_op jit(solution)/shard_map/ppermute | solution.py:409
  16.4 5.1 %collective-permute-start.7 = (f32[72,128]{1,0:T(8,128)S(1)}, f32[72,128]{1,0:T(8,128)S(1)}, u32[]{:S(2)}, u32[]{:S(2)}) collective-permute-start(f32[72,128]{1,0:T(8,128)S(1)} %collective-permute-done.3.er_ref), channel_id=1, source_target_pairs={{0,480},{32,0},{64,32},{96,64},{128,96},{160,128},{192,160},{224,1... | collective-permute-start | bytes 110600 | tf_op jit(solution)/shard_map/ppermute | solution.py:409
  19.9 1.8 %collective-permute-start.5 = (f32[72,128]{1,0:T(8,128)S(1)}, f32[72,128]{1,0:T(8,128)S(1)}, u32[]{:S(2)}, u32[]{:S(2)}) collective-permute-start(f32[72,128]{1,0:T(8,128)S(1)} %collective-permute-done.3.er_ref), channel_id=1, source_target_pairs={{0,32},{32,64},{64,96},{96,128},{128,160},{160,192},{192,224},{224... | collective-permute-start | bytes 110600 | tf_op jit(solution)/shard_map/ppermute | solution.py:409
  19.9 3.7 %collective-permute-start.6 = (f32[72,128]{1,0:T(8,128)S(1)}, f32[72,128]{1,0:T(8,128)S(1)}, u32[]{:S(2)}, u32[]{:S(2)}) collective-permute-start(f32[72,128]{1,0:T(8,128)S(1)} %collective-permute-done.2.el_ref), channel_id=1, source_target_pairs={{0,480},{32,0},{64,32},{96,64},{128,96},{160,128},{192,160},{224,1... | collective-permute-start | bytes 110600 | tf_op jit(solution)/shard_map/ppermute | solution.py:409
  21.5 2.1 %collective-permute-start.4 = (f32[72,128]{1,0:T(8,128)S(1)}, f32[72,128]{1,0:T(8,128)S(1)}, u32[]{:S(2)}, u32[]{:S(2)}) collective-permute-start(f32[72,128]{1,0:T(8,128)S(1)} %collective-permute-done.2.el_ref), channel_id=1, source_target_pairs={{0,32},{32,64},{64,96},{96,128},{128,160},{160,192},{192,224},{224... | collective-permute-start | bytes 110600 | tf_op jit(solution)/shard_map/ppermute | solution.py:409

commit v4 on v3

--- a/solution.py
+++ b/solution.py
@@ -21,7 +21,7 @@
 MSG_KC = MSG_FORCE + 2 * MEM
 MSG_EDGE = MSG_KC + CELLS
 MSG_ROWS = MSG_EDGE + PAD
-PAYLOAD = 5 * COLS
+PAYLOAD = 9 * COLS
 HIGHEST = lax.Precision.HIGHEST
 F32 = jnp.float32
 
@@ -299,26 +299,30 @@
     )
     gram_ref[:, MEM:COLS] = jnp.zeros((PAD, COLS - MEM), F32)
 
+    vec = gram_ref[MEM:PAD, :]
+    sub = lax.broadcasted_iota(jnp.int32, (8, COLS), 0)
+
     def stripe(i):
-        return gram_ref[8 * i : 8 * i + 8, :]
+        block = gram_ref[8 * i : 8 * i + 8, :]
+        block = jnp.where((sub == 7) & (lane >= 8 * i) & (lane < 8 * i + 7), vec, block)
+        return jnp.where((sub == 6) & (lane == 8 * i + 5), roll(vec, -2), block)
 
     def joined(i):
         if i == 0:
             return stripe(0)
-        other = stripe(8 - i)
-        return jnp.where(lane >= 8 * i, stripe(i), roll(other, 8 * i - MEM))
-
-    vec = stripe(8)
-    sub = lax.broadcasted_iota(jnp.int32, (8, COLS), 0)
-    part = jnp.where(sub % 2 == 0, vec, roll(vec, -32))
-    last = jnp.where(lane >= 32, stripe(4), part)
+        return jnp.where(lane >= 8 * i, stripe(i), roll(stripe(8 - i), 8 * i - MEM))
+
     first = jnp.where(lane < MEM, joined(0), roll(joined(1), MEM))
     second = jnp.where(lane < MEM, joined(2), roll(joined(3), MEM))
-    third = jnp.where(
-        lane[0:4] < MEM, last[0:4], roll(last[4:8], MEM)
-    )
-    for c in range(regions):
-        for i, piece in enumerate((first[0:4], first[4:8], second[0:4], second[4:8], third)):
+    middle = stripe(4)
+    third = roll(middle, -32)[0:2]
+    for q in range(1, 4):
+        third = jnp.where(
+            lane[0:2] >= 32 * q, roll(middle, 32 * q - 32)[2 * q : 2 * q + 2], third
+        )
+    pieces = [block[2 * q : 2 * q + 2] for block in (first, second) for q in range(4)]
+    for i, piece in enumerate(pieces + [third]):
+        for c in range(regions):
             pay_ref[c, :, i * COLS : (i + 1) * COLS] = piece
 
 
@@ -328,34 +332,34 @@
     total = pay_ref[0]
     for c in range(1, copies):
         total = total + pay_ref[c]
-    piece = [total[:, i * COLS : (i + 1) * COLS] for i in range(5)]
-    first = jnp.concatenate(piece[0:2], axis=0)
-    second = jnp.concatenate(piece[2:4], axis=0)
-    third = piece[4]
+    piece = [total[:, i * COLS : (i + 1) * COLS] for i in range(9)]
+    first = jnp.concatenate(piece[0:4], axis=0)
+    second = jnp.concatenate(piece[4:8], axis=0)
     halves = [
         first,
         roll(first, MEM),
         second,
         roll(second, MEM),
-        jnp.concatenate([third, roll(third, MEM)], axis=0),
+        jnp.concatenate([roll(piece[8], 32 - 32 * q) for q in range(4)], axis=0),
     ]
+    bvec = jnp.zeros((1, COLS), F32)
     for i in range(8):
         block = halves[i] if i <= 4 else roll(halves[8 - i], MEM - 8 * (8 - i))
-        keep = (lane >= 8 * i) & (lane < MEM)
+        here = lane[0:1] // 8 == i
+        tail = jnp.where(lane[0:1] % 8 == 7, roll(block, 2)[6:7], block[7:8])
+        bvec = jnp.where(here, tail, bvec)
+        keep = (lane >= sub + 8 * i) & (lane < MEM)
         block = jnp.where(keep, block, 0.0)
         block = block + jnp.where(lane == sub + 8 * i, MEM - 1.0, 0.0)
         block = block + jnp.where(lane == sub + (8 * i + MEM), 1.0, 0.0)
         m_ref[8 * i : 8 * i + 8, :] = block
-    tail = halves[4]
-    bvec = jnp.where(
-        lane[0:1] < MEM + 32, roll(tail[0:1, :], MEM), roll(tail[1:2, :], MEM + 32)
-    )
+    bvec = roll(bvec, MEM)
 
     for kb in range(8):
         block = m_ref[8 * kb : 8 * kb + 8, :]
         at = 8 * kb
         full = {
-            (i, j): jnp.broadcast_to(block[i : i + 1, at + j : at + j + 1], (8, COLS))
+            (i, j): jnp.broadcast_to(block[j : j + 1, at + i : at + i + 1], (8, COLS))
             for i in range(8)
             for j in range(i + 1)
         }
@@ -441,7 +445,7 @@
     bel, ber = shift(el, "region", -1), shift(er, "region", -1)
     dev, mean, pay = pl.pallas_call(
         functools.partial(forecast_kernel, regions, tiles),
-        out_shape=(out(MEM, CELLS * COLS), out(CELLS, COLS), out(regions, 4, PAYLOAD)),
+        out_shape=(out(MEM, CELLS * COLS), out(CELLS, COLS), out(regions, 2, PAYLOAD)),
         in_specs=[vmem()] * 11,
         out_specs=(vmem(),) * 3,
         scratch_shapes=[

time: 78.5 us -> 77.7 us (0.990)
  blocking collectives: 42 us -> 40.6 us
    all_to_all x1, blocking collectives: 25.9 us -> 24.7 us  [shards(): lax.all_to_all(jnp.broadcast_to(part, (tiles,) + part.shape), 'tile', 0, 0)]
where the time goes in v4:
time: 77.7 us; the launch traced here: 76.7 us
  blocking collectives  40.6 us (52%)
  starting transfers between devices  17.4 us (22%)
  Pallas kernels  13.2 us (17%)
  local copies, waits for them, and re-layouts  2.7 us (3%)
  waiting for transfers between devices  1.95 us (3%)
    all_to_all x1, blocking collectives, shards(): lax.all_to_all(jnp.broadcast_to(part, (tiles,) + part.shape), 'tile', 0, 0)  24.7 us
    ppermute x8, starting transfers between devices, shift(): return lax.ppermute(x, axis, pairs)  17.4 us
    all_to_all x1, blocking collectives, shards(): part = lax.all_to_all(pay, 'region', 0, 0).sum(axis=0)  15.8 us
    pallas_call x1, Pallas kernels, shards(): pl.pallas_call(functools.partial(forecast_kernel, regions, tiles), out_sh...  7.44 us
    pallas_call x1, Pallas kernels, shards(): pl.pallas_call(functools.partial(analysis_kernel, tiles), out_shape=out(M...  4.9 us
    unnamed x14, local copies, waits for them, and re-layouts  2.62 us
    ppermute x8, waiting for transfers between devices, shift(): return lax.ppermute(x, axis, pairs)  1.95 us
  transfers between devices with their start and end apart: 8, of which 1 were waited for; matrix products, arithmetic and copies ran while one was open for 0% of the time, Pallas kernels for 0%

profile of v4, /device:TPU:1, one launch (start us, length us, event | category | flops | bytes accessed | tf_op | source)
XLA Modules:
  0.0 76.7 jit_solution(3500500291345173)
XLA Ops:
  0.7 0.0 copy-start.4
  0.7 0.0 copy-start.5
  0.7 0.0 copy-start.3
  0.7 0.0 copy-start.6
  0.7 0.6 copy-done.4
  1.3 0.0 copy-done.5
  1.4 0.0 copy-done.3
  1.4 1.0 %copy-done = f32[64,4,4,128]{3,2,1,0:T(4,128)S(1)} copy-done((f32[64,4,4,128]{3,2,1,0:T(4,128)S(1)}, f32[64,4,4,128]{3,2,1,0:T(4,128)}, u32[]{:S(2)}) %copy-start) | copy-done | bytes 524312
  2.4 0.9 %copy-done.1 = f32[64,4,128]{2,1,0:T(4,128)S(1)} copy-done((f32[64,4,128]{2,1,0:T(4,128)S(1)}, f32[64,4,128]{2,1,0:T(4,128)}, u32[]{:S(2)}) %copy-start.1) | copy-done | bytes 131096
  3.3 0.9 %pack.1 = (f32[984,128]{1,0:T(8,128)S(1)}, f32[984,128]{1,0:T(8,128)S(1)}, f32[120,128]{1,0:T(8,128)S(1)}, f32[72,128]{1,0:T(8,128)S(1)}) custom-call(f32[1024,128]{1,0:T(8,128)S(1)} %bitcast.7, f32[256,128]{1,0:T(8,128)S(1)} %bitcast.9, s32[16,128]{1,0:T(8,128)S(1)} %bitcast.11, s32[1,256]{1,0:T(1,128)S(1)} %bitcast.12, f32[1,256]{1,0:T(1,128)S(1)} %bitcast.13, ...), custom_call_target="tpu_custom_call" | custom-call | tf_op jit(solution)/shard_map/pack/pallas_call | solution.py:426
  4.2 2.7 %collective-permute-start = (f32[984,128]{1,0:T(8,128)S(1)}, f32[984,128]{1,0:T(8,128)S(1)}, u32[]{:S(2)}, u32[]{:S(2)}) collective-permute-start(f32[984,128]{1,0:T(8,128)S(1)} %get-tuple-element.13), channel_id=1, source_target_pairs={{0,32},{32,64},{64,96},{96,128},{128,160},{160,192},{192,224},{224... | collective-permute-start | bytes 1511432 | tf_op jit(solution)/shard_map/ppermute | solution.py:413
  6.9 4.2 %collective-permute-start.1 = (f32[984,128]{1,0:T(8,128)S(1)}, f32[984,128]{1,0:T(8,128)S(1)}, u32[]{:S(2)}, u32[]{:S(2)}) collective-permute-start(f32[984,128]{1,0:T(8,128)S(1)} %get-tuple-element.14), channel_id=1, source_target_pairs={{0,480},{32,0},{64,32},{96,64},{128,96},{160,128},{192,160},{224,1... | collective-permute-start | bytes 1511432 | tf_op jit(solution)/shard_map/ppermute | solution.py:413
  11.1 1.3 %collective-permute-start.3 = (f32[72,128]{1,0:T(8,128)S(1)}, f32[72,128]{1,0:T(8,128)S(1)}, u32[]{:S(2)}, u32[]{:S(2)}) collective-permute-start(f32[72,128]{1,0:T(8,128)S(1)} %get-tuple-element.15), channel_id=1, source_target_pairs={{1,0},{2,1},{3,2},{4,3},{5,4},{6,5},{7,6},{8,7},{9,8},{10,9},{11,1... | collective-permute-start | bytes 110600 | tf_op jit(solution)/shard_map/ppermute | solution.py:413
  12.4 4.0 %collective-permute-start.2 = (f32[72,128]{1,0:T(8,128)S(1)}, f32[72,128]{1,0:T(8,128)S(1)}, u32[]{:S(2)}, u32[]{:S(2)}) collective-permute-start(f32[72,128]{1,0:T(8,128)S(1)} %get-tuple-element.15), channel_id=1, source_target_pairs={{0,1},{1,2},{2,3},{3,4},{4,5},{5,6},{6,7},{7,8},{8,9},{9,10},{10,1... | collective-permute-start | bytes 110600 | tf_op jit(solution)/shard_map/ppermute | solution.py:413
  16.4 0.0 collective-permute-done.3.er_ref
  16.4 3.5 %collective-permute-start.7 = (f32[72,128]{1,0:T(8,128)S(1)}, f32[72,128]{1,0:T(8,128)S(1)}, u32[]{:S(2)}, u32[]{:S(2)}) collective-permute-start(f32[72,128]{1,0:T(8,128)S(1)} %collective-permute-done.3.er_ref), channel_id=1, source_target_pairs={{0,480},{32,0},{64,32},{96,64},{128,96},{160,128},{192,160},{224,1... | collective-permute-start | bytes 110600 | tf_op jit(solution)/shard_map/ppermute | solution.py:413
  19.9 0.0 collective-permute-start.5
  19.9 0.0 collective-permute-done.2.el_ref
  19.9 1.6 %collective-permute-start.6 = (f32[72,128]{1,0:T(8,128)S(1)}, f32[72,128]{1,0:T(8,128)S(1)}, u32[]{:S(2)}, u32[]{:S(2)}) collective-permute-start(f32[72,128]{1,0:T(8,128)S(1)} %collective-permute-done.2.el_ref), channel_id=1, source_target_pairs={{0,480},{32,0},{64,32},{96,64},{128,96},{160,128},{192,160},{224,1... | collective-permute-start | bytes 110600 | tf_op jit(solution)/shard_map/ppermute | solution.py:413
  21.5 0.0 collective-permute-done.7.der_ref
  21.5 0.2 collective-permute-start.4
  21.7 0.0 collective-permute-done.5.uer_ref
  21.7 1.9 %collective-permute-done.6.del_ref = f32[72,128]{1,0:T(8,128)S(1)} collective-permute-done((f32[72,128]{1,0:T(8,128)S(1)}, f32[72,128]{1,0:T(8,128)S(1)}, u32[]{:S(2)}, u32[]{:S(2)}) %collective-permute-start.6) | collective-permute-done | bytes 36896 | tf_op jit(solution)/shard_map/ppermute | solution.py:413
  23.6 0.0 collective-permute-done.4.uel_ref
  23.6 0.0 collective-permute-done.above_ref
  23.6 0.0 collective-permute-done.1.below_ref
  23.6 7.4 %forecast.1 = (f32[64,2048]{1,0:T(8,128)S(1)}, f32[16,128]{1,0:T(8,128)S(1)}, f32[16,2,1152]{2,1,0:T(2,128)S(1)}) custom-call(f32[1024,128]{1,0:T(8,128)S(1)} %bitcast.8, f32[256,128]{1,0:T(8,128)S(1)} %bitcast.10, f32[120,128]{1,0:T(8,128)S(1)} %get-tuple-element.12.own_ref, f32[984,128]{1,0:T(8,128)S(1)} %collective-permute-done.above_ref, ...), custom_call_target="tpu_custom_call" | custom-call | tf_op jit(solution)/shard_map/forecast/pallas_call | solution.py:446
  31.1 15.8 %all_to_all.10 = f32[16,2,1152]{2,1,0:T(2,128)S(1)} all-to-all(f32[16,2,1152]{2,1,0:T(2,128)S(1)} %get-tuple-element.16), channel_id=1, replica_groups=mesh['region'=16,'tile'=32] {'region'}, dimensions={0} | all-to-all | bytes 294912 | tf_op jit(solution)/shard_map/all_to_all | solution.py:462
  46.9 0.1 reduce_sum.9
  47.0 0.1 broadcast_in_dim.3
  47.1 24.7 %all_to_all.11.pay_ref = f32[32,2,1152]{2,1,0:T(2,128)S(1)} all-to-all(f32[32,2,1152]{2,1,0:T(2,128)S(1)} %broadcast_in_dim.3), channel_id=1, replica_groups=mesh['region'=16,'tile'=32] {'tile'}, dimensions={0} | all-to-all | bytes 589824 | tf_op jit(solution)/shard_map/all_to_all | solution.py:463
  71.8 4.9 %analysis.1 = f32[1024,128]{1,0:T(8,128)} custom-call(f32[32,2,1152]{2,1,0:T(2,128)S(1)} %all_to_all.11.pay_ref, f32[64,2048]{1,0:T(8,128)S(1)} %get-tuple-element.17.dev_ref, f32[16,128]{1,0:T(8,128)S(1)} %get-tuple-element.18.mean_ref), custom_call_target="tpu_custom_call" | custom-call | tf_op jit(solution)/shard_map/analysis/pallas_call | solution.py:464
  (5 shorter events, 0.0 us)
Async XLA Ops:
  0.0 0.7 copy-start.2
  0.7 0.7 copy-start.4
  0.7 0.7 copy-start.5
  0.7 0.7 copy-start.3
  0.7 0.7 copy-start.6
  1.4 1.0 %copy-start = (f32[64,4,4,128]{3,2,1,0:T(4,128)S(1)}, f32[64,4,4,128]{3,2,1,0:T(4,128)}, u32[]{:S(2)}) copy-start(f32[64,4,4,128]{3,2,1,0:T(4,128)} %param.8) | copy-start | bytes 1572868
  2.4 0.9 %copy-start.1 = (f32[64,4,128]{2,1,0:T(4,128)S(1)}, f32[64,4,128]{2,1,0:T(4,128)}, u32[]{:S(2)}) copy-start(f32[64,4,128]{2,1,0:T(4,128)} %param.9) | copy-start | bytes 393220
  4.2 19.4 %collective-permute-start = (f32[984,128]{1,0:T(8,128)S(1)}, f32[984,128]{1,0:T(8,128)S(1)}, u32[]{:S(2)}, u32[]{:S(2)}) collective-permute-start(f32[984,128]{1,0:T(8,128)S(1)} %get-tuple-element.13), channel_id=1, source_target_pairs={{0,32},{32,64},{64,96},{96,128},{128,160},{160,192},{192,224},{224... | collective-permute-start | bytes 1511432 | tf_op jit(solution)/shard_map/ppermute | solution.py:413
  6.9 16.7 %collective-permute-start.1 = (f32[984,128]{1,0:T(8,128)S(1)}, f32[984,128]{1,0:T(8,128)S(1)}, u32[]{:S(2)}, u32[]{:S(2)}) collective-permute-start(f32[984,128]{1,0:T(8,128)S(1)} %get-tuple-element.14), channel_id=1, source_target_pairs={{0,480},{32,0},{64,32},{96,64},{128,96},{160,128},{192,160},{224,1... | collective-permute-start | bytes 1511432 | tf_op jit(solution)/shard_map/ppermute | solution.py:413
  11.1 5.3 %collective-permute-start.3 = (f32[72,128]{1,0:T(8,128)S(1)}, f32[72,128]{1,0:T(8,128)S(1)}, u32[]{:S(2)}, u32[]{:S(2)}) collective-permute-start(f32[72,128]{1,0:T(8,128)S(1)} %get-tuple-element.15), channel_id=1, source_target_pairs={{1,0},{2,1},{3,2},{4,3},{5,4},{6,5},{7,6},{8,7},{9,8},{10,9},{11,1... | collective-permute-start | bytes 110600 | tf_op jit(solution)/shard_map/ppermute | solution.py:413
  12.4 7.5 %collective-permute-start.2 = (f32[72,128]{1,0:T(8,128)S(1)}, f32[72,128]{1,0:T(8,128)S(1)}, u32[]{:S(2)}, u32[]{:S(2)}) collective-permute-start(f32[72,128]{1,0:T(8,128)S(1)} %get-tuple-element.15), channel_id=1, source_target_pairs={{0,1},{1,2},{2,3},{3,4},{4,5},{5,6},{6,7},{7,8},{8,9},{9,10},{10,1... | collective-permute-start | bytes 110600 | tf_op jit(solution)/shard_map/ppermute | solution.py:413
  16.4 5.1 %collective-permute-start.7 = (f32[72,128]{1,0:T(8,128)S(1)}, f32[72,128]{1,0:T(8,128)S(1)}, u32[]{:S(2)}, u32[]{:S(2)}) collective-permute-start(f32[72,128]{1,0:T(8,128)S(1)} %collective-permute-done.3.er_ref), channel_id=1, source_target_pairs={{0,480},{32,0},{64,32},{96,64},{128,96},{160,128},{192,160},{224,1... | collective-permute-start | bytes 110600 | tf_op jit(solution)/shard_map/ppermute | solution.py:413
  19.9 1.8 %collective-permute-start.5 = (f32[72,128]{1,0:T(8,128)S(1)}, f32[72,128]{1,0:T(8,128)S(1)}, u32[]{:S(2)}, u32[]{:S(2)}) collective-permute-start(f32[72,128]{1,0:T(8,128)S(1)} %collective-permute-done.3.er_ref), channel_id=1, source_target_pairs={{0,32},{32,64},{64,96},{96,128},{128,160},{160,192},{192,224},{224... | collective-permute-start | bytes 110600 | tf_op jit(solution)/shard_map/ppermute | solution.py:413
  19.9 3.7 %collective-permute-start.6 = (f32[72,128]{1,0:T(8,128)S(1)}, f32[72,128]{1,0:T(8,128)S(1)}, u32[]{:S(2)}, u32[]{:S(2)}) collective-permute-start(f32[72,128]{1,0:T(8,128)S(1)} %collective-permute-done.2.el_ref), channel_id=1, source_target_pairs={{0,480},{32,0},{64,32},{96,64},{128,96},{160,128},{192,160},{224,1... | collective-permute-start | bytes 110600 | tf_op jit(solution)/shard_map/ppermute | solution.py:413
  21.5 2.1 %collective-permute-start.4 = (f32[72,128]{1,0:T(8,128)S(1)}, f32[72,128]{1,0:T(8,128)S(1)}, u32[]{:S(2)}, u32[]{:S(2)}) collective-permute-start(f32[72,128]{1,0:T(8,128)S(1)} %collective-permute-done.2.el_ref), channel_id=1, source_target_pairs={{0,32},{32,64},{64,96},{96,128},{128,160},{160,192},{192,224},{224... | collective-permute-start | bytes 110600 | tf_op jit(solution)/shard_map/ppermute | solution.py:413

commit v5 on v4

--- a/solution.py
+++ b/solution.py
@@ -322,7 +322,7 @@
         )
     pieces = [block[2 * q : 2 * q + 2] for block in (first, second) for q in range(4)]
     for i, piece in enumerate(pieces + [third]):
-        for c in range(regions):
+        for c in range(tiles):
             pay_ref[c, :, i * COLS : (i + 1) * COLS] = piece
 
 
@@ -445,7 +445,7 @@
     bel, ber = shift(el, "region", -1), shift(er, "region", -1)
     dev, mean, pay = pl.pallas_call(
         functools.partial(forecast_kernel, regions, tiles),
-        out_shape=(out(MEM, CELLS * COLS), out(CELLS, COLS), out(regions, 2, PAYLOAD)),
+        out_shape=(out(MEM, CELLS * COLS), out(CELLS, COLS), out(tiles, 2, PAYLOAD)),
         in_specs=[vmem()] * 11,
         out_specs=(vmem(),) * 3,
         scratch_shapes=[
@@ -459,10 +459,10 @@
         compiler_params=PARAMS,
         name="forecast",
     )(prior, source, own, above, below, el, er, uel, uer, bel, ber)
-    part = lax.all_to_all(pay, "region", 0, 0).sum(axis=0)
-    pay = lax.all_to_all(jnp.broadcast_to(part, (tiles,) + part.shape), "tile", 0, 0)
+    part = lax.all_to_all(pay, "tile", 0, 0).sum(axis=0)
+    pay = lax.all_to_all(jnp.broadcast_to(part, (regions,) + part.shape), "region", 0, 0)
     result = pl.pallas_call(
-        functools.partial(analysis_kernel, tiles),
+        functools.partial(analysis_kernel, regions),
         out_shape=out(MEM * CELLS, COLS),
         in_specs=[vmem()] * 3,
         out_specs=vmem(),

time: 77.7 us -> 77.3 us (level)
  no operation moved by 1% of the time
where the time goes in v5:
time: 77.3 us; the launch traced here: 77 us
  blocking collectives  40.8 us (53%)
  starting transfers between devices  17.4 us (23%)
  Pallas kernels  13.2 us (17%)
  local copies, waits for them, and re-layouts  2.66 us (3%)
  waiting for transfers between devices  1.95 us (3%)
    all_to_all x1, blocking collectives, shards(): lax.all_to_all(jnp.broadcast_to(part, (regions,) + part.shape), 'region',...  21.2 us
    all_to_all x1, blocking collectives, shards(): part = lax.all_to_all(pay, 'tile', 0, 0).sum(axis=0)  19.7 us
    ppermute x8, starting transfers between devices, shift(): return lax.ppermute(x, axis, pairs)  17.4 us
    pallas_call x1, Pallas kernels, shards(): pl.pallas_call(functools.partial(forecast_kernel, regions, tiles), out_sh...  7.48 us
    pallas_call x1, Pallas kernels, shards(): pl.pallas_call(functools.partial(analysis_kernel, regions), out_shape=out...  4.89 us
    unnamed x14, local copies, waits for them, and re-layouts  2.62 us
    ppermute x8, waiting for transfers between devices, shift(): return lax.ppermute(x, axis, pairs)  1.95 us
  transfers between devices with their start and end apart: 8, of which 1 were waited for; matrix products, arithmetic and copies ran while one was open for 0% of the time, Pallas kernels for 0%

profile of v5, /device:TPU:1, one launch (start us, length us, event | category | flops | bytes accessed | tf_op | source)
XLA Modules:
  0.0 77.0 jit_solution(15064991047908021209)
XLA Ops:
  0.7 0.0 copy-start.4
  0.7 0.0 copy-start.5
  0.7 0.0 copy-start.3
  0.7 0.0 copy-start.6
  0.7 0.0 copy-done.2
  0.7 0.6 copy-done.4
  1.3 0.0 copy-done.5
  1.4 0.0 copy-done.3
  1.4 1.0 %copy-done = f32[64,4,4,128]{3,2,1,0:T(4,128)S(1)} copy-done((f32[64,4,4,128]{3,2,1,0:T(4,128)S(1)}, f32[64,4,4,128]{3,2,1,0:T(4,128)}, u32[]{:S(2)}) %copy-start) | copy-done | bytes 524312
  2.4 0.9 %copy-done.1 = f32[64,4,128]{2,1,0:T(4,128)S(1)} copy-done((f32[64,4,128]{2,1,0:T(4,128)S(1)}, f32[64,4,128]{2,1,0:T(4,128)}, u32[]{:S(2)}) %copy-start.1) | copy-done | bytes 131096
  3.3 0.9 %pack.1 = (f32[984,128]{1,0:T(8,128)S(1)}, f32[984,128]{1,0:T(8,128)S(1)}, f32[120,128]{1,0:T(8,128)S(1)}, f32[72,128]{1,0:T(8,128)S(1)}) custom-call(f32[1024,128]{1,0:T(8,128)S(1)} %bitcast.7, f32[256,128]{1,0:T(8,128)S(1)} %bitcast.9, s32[16,128]{1,0:T(8,128)S(1)} %bitcast.11, s32[1,256]{1,0:T(1,128)S(1)} %bitcast.12, f32[1,256]{1,0:T(1,128)S(1)} %bitcast.13, ...), custom_call_target="tpu_custom_call" | custom-call | tf_op jit(solution)/shard_map/pack/pallas_call | solution.py:426
  4.2 2.7 %collective-permute-start = (f32[984,128]{1,0:T(8,128)S(1)}, f32[984,128]{1,0:T(8,128)S(1)}, u32[]{:S(2)}, u32[]{:S(2)}) collective-permute-start(f32[984,128]{1,0:T(8,128)S(1)} %get-tuple-element.13), channel_id=1, source_target_pairs={{0,32},{32,64},{64,96},{96,128},{128,160},{160,192},{192,224},{224... | collective-permute-start | bytes 1511432 | tf_op jit(solution)/shard_map/ppermute | solution.py:413
  6.9 4.2 %collective-permute-start.1 = (f32[984,128]{1,0:T(8,128)S(1)}, f32[984,128]{1,0:T(8,128)S(1)}, u32[]{:S(2)}, u32[]{:S(2)}) collective-permute-start(f32[984,128]{1,0:T(8,128)S(1)} %get-tuple-element.14), channel_id=1, source_target_pairs={{0,480},{32,0},{64,32},{96,64},{128,96},{160,128},{192,160},{224,1... | collective-permute-start | bytes 1511432 | tf_op jit(solution)/shard_map/ppermute | solution.py:413
  11.1 1.3 %collective-permute-start.3 = (f32[72,128]{1,0:T(8,128)S(1)}, f32[72,128]{1,0:T(8,128)S(1)}, u32[]{:S(2)}, u32[]{:S(2)}) collective-permute-start(f32[72,128]{1,0:T(8,128)S(1)} %get-tuple-element.15), channel_id=1, source_target_pairs={{1,0},{2,1},{3,2},{4,3},{5,4},{6,5},{7,6},{8,7},{9,8},{10,9},{11,1... | collective-permute-start | bytes 110600 | tf_op jit(solution)/shard_map/ppermute | solution.py:413
  12.4 4.0 %collective-permute-start.2 = (f32[72,128]{1,0:T(8,128)S(1)}, f32[72,128]{1,0:T(8,128)S(1)}, u32[]{:S(2)}, u32[]{:S(2)}) collective-permute-start(f32[72,128]{1,0:T(8,128)S(1)} %get-tuple-element.15), channel_id=1, source_target_pairs={{0,1},{1,2},{2,3},{3,4},{4,5},{5,6},{6,7},{7,8},{8,9},{9,10},{10,1... | collective-permute-start | bytes 110600 | tf_op jit(solution)/shard_map/ppermute | solution.py:413
  16.4 0.0 collective-permute-done.3.er_ref
  16.4 3.5 %collective-permute-start.7 = (f32[72,128]{1,0:T(8,128)S(1)}, f32[72,128]{1,0:T(8,128)S(1)}, u32[]{:S(2)}, u32[]{:S(2)}) collective-permute-start(f32[72,128]{1,0:T(8,128)S(1)} %collective-permute-done.3.er_ref), channel_id=1, source_target_pairs={{0,480},{32,0},{64,32},{96,64},{128,96},{160,128},{192,160},{224,1... | collective-permute-start | bytes 110600 | tf_op jit(solution)/shard_map/ppermute | solution.py:413
  19.9 0.0 collective-permute-start.5
  19.9 0.0 collective-permute-done.2.el_ref
  19.9 1.6 %collective-permute-start.6 = (f32[72,128]{1,0:T(8,128)S(1)}, f32[72,128]{1,0:T(8,128)S(1)}, u32[]{:S(2)}, u32[]{:S(2)}) collective-permute-start(f32[72,128]{1,0:T(8,128)S(1)} %collective-permute-done.2.el_ref), channel_id=1, source_target_pairs={{0,480},{32,0},{64,32},{96,64},{128,96},{160,128},{192,160},{224,1... | collective-permute-start | bytes 110600 | tf_op jit(solution)/shard_map/ppermute | solution.py:413
  21.5 0.0 collective-permute-done.7.der_ref
  21.5 0.2 collective-permute-start.4
  21.7 0.0 collective-permute-done.5.uer_ref
  21.7 1.9 %collective-permute-done.6.del_ref = f32[72,128]{1,0:T(8,128)S(1)} collective-permute-done((f32[72,128]{1,0:T(8,128)S(1)}, f32[72,128]{1,0:T(8,128)S(1)}, u32[]{:S(2)}, u32[]{:S(2)}) %collective-permute-start.6) | collective-permute-done | bytes 36896 | tf_op jit(solution)/shard_map/ppermute | solution.py:413
  23.6 0.0 collective-permute-done.4.uel_ref
  23.6 0.0 collective-permute-done.above_ref
  23.6 0.0 collective-permute-done.1.below_ref
  23.6 7.5 %forecast.1 = (f32[64,2048]{1,0:T(8,128)S(1)}, f32[16,128]{1,0:T(8,128)S(1)}, f32[32,2,1152]{2,1,0:T(2,128)S(1)}) custom-call(f32[1024,128]{1,0:T(8,128)S(1)} %bitcast.8, f32[256,128]{1,0:T(8,128)S(1)} %bitcast.10, f32[120,128]{1,0:T(8,128)S(1)} %get-tuple-element.12.own_ref, f32[984,128]{1,0:T(8,128)S(1)} %collective-permute-done.above_ref, ...), custom_call_target="tpu_custom_call" | custom-call | tf_op jit(solution)/shard_map/forecast/pallas_call | solution.py:446
  31.1 19.7 %all_to_all.10 = f32[32,2,1152]{2,1,0:T(2,128)S(1)} all-to-all(f32[32,2,1152]{2,1,0:T(2,128)S(1)} %get-tuple-element.16), channel_id=1, replica_groups=mesh['region'=16,'tile'=32] {'tile'}, dimensions={0} | all-to-all | bytes 589824 | tf_op jit(solution)/shard_map/all_to_all | solution.py:462
  50.8 0.1 reduce_sum.9
  50.9 21.2 %all_to_all.11.pay_ref = f32[16,2,1152]{2,1,0:T(2,128)S(1)} all-to-all(f32[16,2,1152]{2,1,0:T(2,128)S(1)} %broadcast_in_dim.3), channel_id=1, replica_groups=mesh['region'=16,'tile'=32] {'region'}, dimensions={0} | all-to-all | bytes 294912 | tf_op jit(solution)/shard_map/all_to_all | solution.py:463
  72.1 4.9 %analysis.1 = f32[1024,128]{1,0:T(8,128)} custom-call(f32[16,2,1152]{2,1,0:T(2,128)S(1)} %all_to_all.11.pay_ref, f32[64,2048]{1,0:T(8,128)S(1)} %get-tuple-element.17.dev_ref, f32[16,128]{1,0:T(8,128)S(1)} %get-tuple-element.18.mean_ref), custom_call_target="tpu_custom_call" | custom-call | tf_op jit(solution)/shard_map/analysis/pallas_call | solution.py:464
  (5 shorter events, 0.0 us)
Async XLA Ops:
  0.0 0.7 copy-start.2
  0.7 0.7 copy-start.4
  0.7 0.7 copy-start.5
  0.7 0.7 copy-start.3
  0.7 0.7 copy-start.6
  1.4 1.0 %copy-start = (f32[64,4,4,128]{3,2,1,0:T(4,128)S(1)}, f32[64,4,4,128]{3,2,1,0:T(4,128)}, u32[]{:S(2)}) copy-start(f32[64,4,4,128]{3,2,1,0:T(4,128)} %param.8) | copy-start | bytes 1572868
  2.4 0.9 %copy-start.1 = (f32[64,4,128]{2,1,0:T(4,128)S(1)}, f32[64,4,128]{2,1,0:T(4,128)}, u32[]{:S(2)}) copy-start(f32[64,4,128]{2,1,0:T(4,128)} %param.9) | copy-start | bytes 393220
  4.2 19.4 %collective-permute-start = (f32[984,128]{1,0:T(8,128)S(1)}, f32[984,128]{1,0:T(8,128)S(1)}, u32[]{:S(2)}, u32[]{:S(2)}) collective-permute-start(f32[984,128]{1,0:T(8,128)S(1)} %get-tuple-element.13), channel_id=1, source_target_pairs={{0,32},{32,64},{64,96},{96,128},{128,160},{160,192},{192,224},{224... | collective-permute-start | bytes 1511432 | tf_op jit(solution)/shard_map/ppermute | solution.py:413
  6.9 16.7 %collective-permute-start.1 = (f32[984,128]{1,0:T(8,128)S(1)}, f32[984,128]{1,0:T(8,128)S(1)}, u32[]{:S(2)}, u32[]{:S(2)}) collective-permute-start(f32[984,128]{1,0:T(8,128)S(1)} %get-tuple-element.14), channel_id=1, source_target_pairs={{0,480},{32,0},{64,32},{96,64},{128,96},{160,128},{192,160},{224,1... | collective-permute-start | bytes 1511432 | tf_op jit(solution)/shard_map/ppermute | solution.py:413
  11.1 5.3 %collective-permute-start.3 = (f32[72,128]{1,0:T(8,128)S(1)}, f32[72,128]{1,0:T(8,128)S(1)}, u32[]{:S(2)}, u32[]{:S(2)}) collective-permute-start(f32[72,128]{1,0:T(8,128)S(1)} %get-tuple-element.15), channel_id=1, source_target_pairs={{1,0},{2,1},{3,2},{4,3},{5,4},{6,5},{7,6},{8,7},{9,8},{10,9},{11,1... | collective-permute-start | bytes 110600 | tf_op jit(solution)/shard_map/ppermute | solution.py:413
  12.4 7.5 %collective-permute-start.2 = (f32[72,128]{1,0:T(8,128)S(1)}, f32[72,128]{1,0:T(8,128)S(1)}, u32[]{:S(2)}, u32[]{:S(2)}) collective-permute-start(f32[72,128]{1,0:T(8,128)S(1)} %get-tuple-element.15), channel_id=1, source_target_pairs={{0,1},{1,2},{2,3},{3,4},{4,5},{5,6},{6,7},{7,8},{8,9},{9,10},{10,1... | collective-permute-start | bytes 110600 | tf_op jit(solution)/shard_map/ppermute | solution.py:413
  16.4 5.1 %collective-permute-start.7 = (f32[72,128]{1,0:T(8,128)S(1)}, f32[72,128]{1,0:T(8,128)S(1)}, u32[]{:S(2)}, u32[]{:S(2)}) collective-permute-start(f32[72,128]{1,0:T(8,128)S(1)} %collective-permute-done.3.er_ref), channel_id=1, source_target_pairs={{0,480},{32,0},{64,32},{96,64},{128,96},{160,128},{192,160},{224,1... | collective-permute-start | bytes 110600 | tf_op jit(solution)/shard_map/ppermute | solution.py:413
  19.9 1.8 %collective-permute-start.5 = (f32[72,128]{1,0:T(8,128)S(1)}, f32[72,128]{1,0:T(8,128)S(1)}, u32[]{:S(2)}, u32[]{:S(2)}) collective-permute-start(f32[72,128]{1,0:T(8,128)S(1)} %collective-permute-done.3.er_ref), channel_id=1, source_target_pairs={{0,32},{32,64},{64,96},{96,128},{128,160},{160,192},{192,224},{224... | collective-permute-start | bytes 110600 | tf_op jit(solution)/shard_map/ppermute | solution.py:413
  19.9 3.7 %collective-permute-start.6 = (f32[72,128]{1,0:T(8,128)S(1)}, f32[72,128]{1,0:T(8,128)S(1)}, u32[]{:S(2)}, u32[]{:S(2)}) collective-permute-start(f32[72,128]{1,0:T(8,128)S(1)} %collective-permute-done.2.el_ref), channel_id=1, source_target_pairs={{0,480},{32,0},{64,32},{96,64},{128,96},{160,128},{192,160},{224,1... | collective-permute-start | bytes 110600 | tf_op jit(solution)/shard_map/ppermute | solution.py:413
  21.5 2.1 %collective-permute-start.4 = (f32[72,128]{1,0:T(8,128)S(1)}, f32[72,128]{1,0:T(8,128)S(1)}, u32[]{:S(2)}, u32[]{:S(2)}) collective-permute-start(f32[72,128]{1,0:T(8,128)S(1)} %collective-permute-done.2.el_ref), channel_id=1, source_target_pairs={{0,32},{32,64},{64,96},{96,128},{128,160},{160,192},{192,224},{224... | collective-permute-start | bytes 110600 | tf_op jit(solution)/shard_map/ppermute | solution.py:413

commit v6 on v5

--- a/solution.py
+++ b/solution.py
@@ -388,12 +388,14 @@
     y = jnp.sum(inverse * bvec, axis=1, keepdims=True)
     w = jnp.sum(inverse * y, axis=0, keepdims=True)
     blend = (inverse * jnp.sqrt(jnp.full((1, COLS), MEM - 1.0, F32)) + w)[:, MEM:COLS]
-    for lr in range(CELLS):
-        cols = slice(lr * COLS, (lr + 1) * COLS)
-        value = mean_ref[lr : lr + 1, :] + jnp.dot(
-            blend, dev_ref[:, cols], precision=HIGHEST, preferred_element_type=F32
+    for lr in range(0, CELLS, 2):
+        both = jnp.dot(
+            blend, dev_ref[:, lr * COLS : (lr + 2) * COLS],
+            precision=HIGHEST, preferred_element_type=F32,
         )
-        out_ref[pl.ds(lr, MEM, stride=CELLS), :] = value
+        for i in range(2):
+            value = mean_ref[lr + i : lr + i + 1, :] + both[:, i * COLS : (i + 1) * COLS]
+            out_ref[pl.ds(lr + i, MEM, stride=CELLS), :] = value
 
 
 def vmem():

time: 77.3 us -> 77.3 us (level)
  no operation moved by 1% of the time
where the time goes in v6:
time: 77.3 us; the launch traced here: 77 us
  blocking collectives  40.8 us (53%)
  starting transfers between devices  17.4 us (23%)
  Pallas kernels  13.2 us (17%)
  local copies, waits for them, and re-layouts  2.66 us (3%)
  waiting for transfers between devices  1.95 us (3%)
    all_to_all x1, blocking collectives, shards(): lax.all_to_all(jnp.broadcast_to(part, (regions,) + part.shape), 'region',...  21.2 us
    all_to_all x1, blocking collectives, shards(): part = lax.all_to_all(pay, 'tile', 0, 0).sum(axis=0)  19.7 us
    ppermute x8, starting transfers between devices, shift(): return lax.ppermute(x, axis, pairs)  17.4 us
    pallas_call x1, Pallas kernels, shards(): pl.pallas_call(functools.partial(forecast_kernel, regions, tiles), out_sh...  7.48 us
    pallas_call x1, Pallas kernels, shards(): pl.pallas_call(functools.partial(analysis_kernel, regions), out_shape=out...  4.88 us
    unnamed x14, local copies, waits for them, and re-layouts  2.62 us
    ppermute x8, waiting for transfers between devices, shift(): return lax.ppermute(x, axis, pairs)  1.95 us
  transfers between devices with their start and end apart: 8, of which 1 were waited for; matrix products, arithmetic and copies ran while one was open for 0% of the time, Pallas kernels for 0%

profile of v6, /device:TPU:1, one launch (start us, length us, event | category | flops | bytes accessed | tf_op | source)
XLA Modules:
  0.0 77.0 jit_solution(7391216824790768834)
XLA Ops:
  0.7 0.0 copy-start.4
  0.7 0.0 copy-start.5
  0.7 0.0 copy-start.3
  0.7 0.0 copy-start.6
  0.7 0.6 copy-done.4
  1.3 0.0 copy-done.5
  1.4 0.0 copy-done.3
  1.4 0.0 copy-done.6
  1.4 1.0 %copy-done = f32[64,4,4,128]{3,2,1,0:T(4,128)S(1)} copy-done((f32[64,4,4,128]{3,2,1,0:T(4,128)S(1)}, f32[64,4,4,128]{3,2,1,0:T(4,128)}, u32[]{:S(2)}) %copy-start) | copy-done | bytes 524312
  2.4 0.9 %copy-done.1 = f32[64,4,128]{2,1,0:T(4,128)S(1)} copy-done((f32[64,4,128]{2,1,0:T(4,128)S(1)}, f32[64,4,128]{2,1,0:T(4,128)}, u32[]{:S(2)}) %copy-start.1) | copy-done | bytes 131096
  3.3 0.9 %pack.1 = (f32[984,128]{1,0:T(8,128)S(1)}, f32[984,128]{1,0:T(8,128)S(1)}, f32[120,128]{1,0:T(8,128)S(1)}, f32[72,128]{1,0:T(8,128)S(1)}) custom-call(f32[1024,128]{1,0:T(8,128)S(1)} %bitcast.7, f32[256,128]{1,0:T(8,128)S(1)} %bitcast.9, s32[16,128]{1,0:T(8,128)S(1)} %bitcast.11, s32[1,256]{1,0:T(1,128)S(1)} %bitcast.12, f32[1,256]{1,0:T(1,128)S(1)} %bitcast.13, ...), custom_call_target="tpu_custom_call" | custom-call | tf_op jit(solution)/shard_map/pack/pallas_call | solution.py:428
  4.2 2.7 %collective-permute-start = (f32[984,128]{1,0:T(8,128)S(1)}, f32[984,128]{1,0:T(8,128)S(1)}, u32[]{:S(2)}, u32[]{:S(2)}) collective-permute-start(f32[984,128]{1,0:T(8,128)S(1)} %get-tuple-element.13), channel_id=1, source_target_pairs={{0,32},{32,64},{64,96},{96,128},{128,160},{160,192},{192,224},{224... | collective-permute-start | bytes 1511432 | tf_op jit(solution)/shard_map/ppermute | solution.py:415
  6.9 4.2 %collective-permute-start.1 = (f32[984,128]{1,0:T(8,128)S(1)}, f32[984,128]{1,0:T(8,128)S(1)}, u32[]{:S(2)}, u32[]{:S(2)}) collective-permute-start(f32[984,128]{1,0:T(8,128)S(1)} %get-tuple-element.14), channel_id=1, source_target_pairs={{0,480},{32,0},{64,32},{96,64},{128,96},{160,128},{192,160},{224,1... | collective-permute-start | bytes 1511432 | tf_op jit(solution)/shard_map/ppermute | solution.py:415
  11.1 1.3 %collective-permute-start.3 = (f32[72,128]{1,0:T(8,128)S(1)}, f32[72,128]{1,0:T(8,128)S(1)}, u32[]{:S(2)}, u32[]{:S(2)}) collective-permute-start(f32[72,128]{1,0:T(8,128)S(1)} %get-tuple-element.15), channel_id=1, source_target_pairs={{1,0},{2,1},{3,2},{4,3},{5,4},{6,5},{7,6},{8,7},{9,8},{10,9},{11,1... | collective-permute-start | bytes 110600 | tf_op jit(solution)/shard_map/ppermute | solution.py:415
  12.4 4.0 %collective-permute-start.2 = (f32[72,128]{1,0:T(8,128)S(1)}, f32[72,128]{1,0:T(8,128)S(1)}, u32[]{:S(2)}, u32[]{:S(2)}) collective-permute-start(f32[72,128]{1,0:T(8,128)S(1)} %get-tuple-element.15), channel_id=1, source_target_pairs={{0,1},{1,2},{2,3},{3,4},{4,5},{5,6},{6,7},{7,8},{8,9},{9,10},{10,1... | collective-permute-start | bytes 110600 | tf_op jit(solution)/shard_map/ppermute | solution.py:415
  16.4 0.0 collective-permute-done.3.er_ref
  16.4 3.5 %collective-permute-start.7 = (f32[72,128]{1,0:T(8,128)S(1)}, f32[72,128]{1,0:T(8,128)S(1)}, u32[]{:S(2)}, u32[]{:S(2)}) collective-permute-start(f32[72,128]{1,0:T(8,128)S(1)} %collective-permute-done.3.er_ref), channel_id=1, source_target_pairs={{0,480},{32,0},{64,32},{96,64},{128,96},{160,128},{192,160},{224,1... | collective-permute-start | bytes 110600 | tf_op jit(solution)/shard_map/ppermute | solution.py:415
  19.9 0.0 collective-permute-start.5
  19.9 0.0 collective-permute-done.2.el_ref
  19.9 1.6 %collective-permute-start.6 = (f32[72,128]{1,0:T(8,128)S(1)}, f32[72,128]{1,0:T(8,128)S(1)}, u32[]{:S(2)}, u32[]{:S(2)}) collective-permute-start(f32[72,128]{1,0:T(8,128)S(1)} %collective-permute-done.2.el_ref), channel_id=1, source_target_pairs={{0,480},{32,0},{64,32},{96,64},{128,96},{160,128},{192,160},{224,1... | collective-permute-start | bytes 110600 | tf_op jit(solution)/shard_map/ppermute | solution.py:415
  21.5 0.0 collective-permute-done.7.der_ref
  21.5 0.2 collective-permute-start.4
  21.7 0.0 collective-permute-done.5.uer_ref
  21.7 1.9 %collective-permute-done.6.del_ref = f32[72,128]{1,0:T(8,128)S(1)} collective-permute-done((f32[72,128]{1,0:T(8,128)S(1)}, f32[72,128]{1,0:T(8,128)S(1)}, u32[]{:S(2)}, u32[]{:S(2)}) %collective-permute-start.6) | collective-permute-done | bytes 36896 | tf_op jit(solution)/shard_map/ppermute | solution.py:415
  23.6 0.0 collective-permute-done.4.uel_ref
  23.6 0.0 collective-permute-done.above_ref
  23.6 0.0 collective-permute-done.1.below_ref
  23.6 7.5 %forecast.1 = (f32[64,2048]{1,0:T(8,128)S(1)}, f32[16,128]{1,0:T(8,128)S(1)}, f32[32,2,1152]{2,1,0:T(2,128)S(1)}) custom-call(f32[1024,128]{1,0:T(8,128)S(1)} %bitcast.8, f32[256,128]{1,0:T(8,128)S(1)} %bitcast.10, f32[120,128]{1,0:T(8,128)S(1)} %get-tuple-element.12.own_ref, f32[984,128]{1,0:T(8,128)S(1)} %collective-permute-done.above_ref, ...), custom_call_target="tpu_custom_call" | custom-call | tf_op jit(solution)/shard_map/forecast/pallas_call | solution.py:448
  31.1 19.7 %all_to_all.10 = f32[32,2,1152]{2,1,0:T(2,128)S(1)} all-to-all(f32[32,2,1152]{2,1,0:T(2,128)S(1)} %get-tuple-element.16), channel_id=1, replica_groups=mesh['region'=16,'tile'=32] {'tile'}, dimensions={0} | all-to-all | bytes 589824 | tf_op jit(solution)/shard_map/all_to_all | solution.py:464
  50.8 0.1 reduce_sum.9
  50.9 21.2 %all_to_all.11.pay_ref = f32[16,2,1152]{2,1,0:T(2,128)S(1)} all-to-all(f32[16,2,1152]{2,1,0:T(2,128)S(1)} %broadcast_in_dim.3), channel_id=1, replica_groups=mesh['region'=16,'tile'=32] {'region'}, dimensions={0} | all-to-all | bytes 294912 | tf_op jit(solution)/shard_map/all_to_all | solution.py:465
  72.1 4.9 %analysis.1 = f32[1024,128]{1,0:T(8,128)} custom-call(f32[16,2,1152]{2,1,0:T(2,128)S(1)} %all_to_all.11.pay_ref, f32[64,2048]{1,0:T(8,128)S(1)} %get-tuple-element.17.dev_ref, f32[16,128]{1,0:T(8,128)S(1)} %get-tuple-element.18.mean_ref), custom_call_target="tpu_custom_call" | custom-call | tf_op jit(solution)/shard_map/analysis/pallas_call | solution.py:466
  (5 shorter events, 0.0 us)
Async XLA Ops:
  0.0 0.7 copy-start.2
  0.7 0.7 copy-start.4
  0.7 0.7 copy-start.5
  0.7 0.7 copy-start.3
  0.7 0.7 copy-start.6
  1.4 1.0 %copy-start = (f32[64,4,4,128]{3,2,1,0:T(4,128)S(1)}, f32[64,4,4,128]{3,2,1,0:T(4,128)}, u32[]{:S(2)}) copy-start(f32[64,4,4,128]{3,2,1,0:T(4,128)} %param.8) | copy-start | bytes 1572868
  2.4 0.9 %copy-start.1 = (f32[64,4,128]{2,1,0:T(4,128)S(1)}, f32[64,4,128]{2,1,0:T(4,128)}, u32[]{:S(2)}) copy-start(f32[64,4,128]{2,1,0:T(4,128)} %param.9) | copy-start | bytes 393220
  4.2 19.4 %collective-permute-start = (f32[984,128]{1,0:T(8,128)S(1)}, f32[984,128]{1,0:T(8,128)S(1)}, u32[]{:S(2)}, u32[]{:S(2)}) collective-permute-start(f32[984,128]{1,0:T(8,128)S(1)} %get-tuple-element.13), channel_id=1, source_target_pairs={{0,32},{32,64},{64,96},{96,128},{128,160},{160,192},{192,224},{224... | collective-permute-start | bytes 1511432 | tf_op jit(solution)/shard_map/ppermute | solution.py:415
  6.9 16.7 %collective-permute-start.1 = (f32[984,128]{1,0:T(8,128)S(1)}, f32[984,128]{1,0:T(8,128)S(1)}, u32[]{:S(2)}, u32[]{:S(2)}) collective-permute-start(f32[984,128]{1,0:T(8,128)S(1)} %get-tuple-element.14), channel_id=1, source_target_pairs={{0,480},{32,0},{64,32},{96,64},{128,96},{160,128},{192,160},{224,1... | collective-permute-start | bytes 1511432 | tf_op jit(solution)/shard_map/ppermute | solution.py:415
  11.1 5.3 %collective-permute-start.3 = (f32[72,128]{1,0:T(8,128)S(1)}, f32[72,128]{1,0:T(8,128)S(1)}, u32[]{:S(2)}, u32[]{:S(2)}) collective-permute-start(f32[72,128]{1,0:T(8,128)S(1)} %get-tuple-element.15), channel_id=1, source_target_pairs={{1,0},{2,1},{3,2},{4,3},{5,4},{6,5},{7,6},{8,7},{9,8},{10,9},{11,1... | collective-permute-start | bytes 110600 | tf_op jit(solution)/shard_map/ppermute | solution.py:415
  12.4 7.5 %collective-permute-start.2 = (f32[72,128]{1,0:T(8,128)S(1)}, f32[72,128]{1,0:T(8,128)S(1)}, u32[]{:S(2)}, u32[]{:S(2)}) collective-permute-start(f32[72,128]{1,0:T(8,128)S(1)} %get-tuple-element.15), channel_id=1, source_target_pairs={{0,1},{1,2},{2,3},{3,4},{4,5},{5,6},{6,7},{7,8},{8,9},{9,10},{10,1... | collective-permute-start | bytes 110600 | tf_op jit(solution)/shard_map/ppermute | solution.py:415
  16.4 5.1 %collective-permute-start.7 = (f32[72,128]{1,0:T(8,128)S(1)}, f32[72,128]{1,0:T(8,128)S(1)}, u32[]{:S(2)}, u32[]{:S(2)}) collective-permute-start(f32[72,128]{1,0:T(8,128)S(1)} %collective-permute-done.3.er_ref), channel_id=1, source_target_pairs={{0,480},{32,0},{64,32},{96,64},{128,96},{160,128},{192,160},{224,1... | collective-permute-start | bytes 110600 | tf_op jit(solution)/shard_map/ppermute | solution.py:415
  19.9 1.8 %collective-permute-start.5 = (f32[72,128]{1,0:T(8,128)S(1)}, f32[72,128]{1,0:T(8,128)S(1)}, u32[]{:S(2)}, u32[]{:S(2)}) collective-permute-start(f32[72,128]{1,0:T(8,128)S(1)} %collective-permute-done.3.er_ref), channel_id=1, source_target_pairs={{0,32},{32,64},{64,96},{96,128},{128,160},{160,192},{192,224},{224... | collective-permute-start | bytes 110600 | tf_op jit(solution)/shard_map/ppermute | solution.py:415
  19.9 3.7 %collective-permute-start.6 = (f32[72,128]{1,0:T(8,128)S(1)}, f32[72,128]{1,0:T(8,128)S(1)}, u32[]{:S(2)}, u32[]{:S(2)}) collective-permute-start(f32[72,128]{1,0:T(8,128)S(1)} %collective-permute-done.2.el_ref), channel_id=1, source_target_pairs={{0,480},{32,0},{64,32},{96,64},{128,96},{160,128},{192,160},{224,1... | collective-permute-start | bytes 110600 | tf_op jit(solution)/shard_map/ppermute | solution.py:415
  21.5 2.1 %collective-permute-start.4 = (f32[72,128]{1,0:T(8,128)S(1)}, f32[72,128]{1,0:T(8,128)S(1)}, u32[]{:S(2)}, u32[]{:S(2)}) collective-permute-start(f32[72,128]{1,0:T(8,128)S(1)} %collective-permute-done.2.el_ref), channel_id=1, source_target_pairs={{0,32},{32,64},{64,96},{96,128},{128,160},{160,192},{192,224},{224... | collective-permute-start | bytes 110600 | tf_op jit(solution)/shard_map/ppermute | solution.py:415
